TPU v7x, 512 devices: a whole 4x8x8 slice. The times are simulated.
512 devices in a mesh: rows: 16 (over z, core), cols: 32 (over y, x).
Axes of the slice: x: 4, y: 8, z: 8, core: 2. Of those that a mesh axis runs over, the one named last changes fastest.
Arguments:
- genotypes: bfloat16 [491520, 2048], P(('rows', 'cols')), may hold values from 0 to 2
- probes: bfloat16 [491520, 128], P(('rows', 'cols')), may hold values from -6 to 6
- missing_codes: int32 [491520], P(('rows', 'cols')), may hold values from 0 to 31
Outputs:
- basis: bfloat16 [491520, 128], P(('rows', 'cols'))
- scores: bfloat16 [2048, 128], replicated
Inputs may be any that keep to these rules, and one draw needn't show every extreme that they name: `missing_codes`: A code c below 16 marks SNPs c * 128 to (c + 1) * 128 - 1 as missing for that individual; larger codes mark none.
All inputs are finite; a program needn't handle non-finite values.
Results may differ from a plain program's by a relative error of at most 0.017.
Values sent between devices are 32-bit elements; how exact they have to be, the bound alone decides.
No kernel may reach another device: no remote copies, remote signals or barrier semaphores. Data moves between devices by JAX's collectives and lax.ppermute only.
A program may use at most 64 MiB of HBM per device.

v0:
```python
import math

import jax
import jax.numpy as jnp
from jax import lax
from jax.sharding import Mesh
from jax.sharding import PartitionSpec as P

BLOCK_SNPS = 128
ROWS_COLS = ("rows_0", "rows_1", "cols_0", "cols_1")
ROWS = ("rows_0", "rows_1")
COLS = ("cols_0", "cols_1")


def split_up(array, dim, size):
    lengths = array.shape
    blocks = array.reshape(*lengths[:dim], size, lengths[dim] // size, *lengths[dim + 1 :])
    return jnp.moveaxis(blocks, dim, 0)


def sum_at_owner(array, axis, dim):
    blocks = split_up(array, dim, lax.axis_size(axis))
    arrived = lax.all_to_all(blocks, axis, split_axis=0, concat_axis=0, tiled=True)
    return arrived.sum(axis=0)


def summed_rows(array, axes, dim):
    far, near = axes
    own = sum_at_owner(split_up(array, dim, lax.axis_size(far)), near, dim + 1)
    return jnp.sum(lax.all_to_all(own, far, 0, 0, tiled=True), axis=0)


def rows_for(lines, size):
    spare = -lines.shape[0] % size
    if not spare:
        return lines
    return jnp.concatenate([lines, jnp.zeros((spare, *lines.shape[1:]), lines.dtype)])


def sent_to_all(array, axis):
    size = lax.axis_size(axis)
    return lax.all_to_all(
        jnp.broadcast_to(array[None], (size, *array.shape)), axis, 0, 0, tiled=True
    )


def joined_along(blocks, dim):
    lengths = list(blocks.shape[1:])
    lengths[dim] *= blocks.shape[0]
    return jnp.moveaxis(blocks, 0, dim).reshape(lengths)


def gathered_by_axis(array, axes, dim):
    far, near = axes
    first = sent_to_all(array, far)
    blocks = jnp.swapaxes(sent_to_all(first, near), 0, 1)
    return joined_along(blocks.reshape(-1, *array.shape), dim)


def sum_by_parts(array, axes):
    lines = array.reshape(-1)
    own = summed_rows(rows_for(lines, lax.axis_size(axes[0]) * lax.axis_size(axes[1])), axes, 0)
    whole = gathered_by_axis(own, axes, 0)
    return whole[: len(lines)].reshape(array.shape)


def everywhere(values):
    return jax.tree.map(
        lambda part: sum_by_parts(part, ("rows_0", ("rows_1", "cols_0", "cols_1"))), values
    )


def statistics(moments):
    counted = jnp.maximum(moments[0], 1.0)
    mean = moments[1] / counted
    inv_sd = 1.0 / jnp.sqrt(moments[2] / counted - mean * mean + 1e-05)
    return (mean, inv_sd)


def per_device(genotypes, probes, missing_codes):
    snps = genotypes.shape[1]
    total_rows = genotypes.shape[0] * lax.axis_size(ROWS) * lax.axis_size(COLS)
    snp_block = jnp.arange(snps) // BLOCK_SNPS
    observed = (snp_block[None, :] != missing_codes[:, None]).astype(jnp.float32)
    dosage = genotypes.astype(jnp.float32) * observed
    moments = jnp.stack([jnp.sum(observed, 0), jnp.sum(dosage, 0), jnp.sum(dosage * dosage, 0)])
    moments = everywhere(moments)
    mean, inv_sd = statistics(moments)
    standard = (
        (genotypes.astype(jnp.float32) - mean[None, :]) * inv_sd[None, :] * observed
    ).astype(jnp.bfloat16)
    partial_proj = jnp.einsum("rs,rb->sb", standard, probes, preferred_element_type=jnp.float32)
    projection = everywhere(partial_proj) / math.sqrt(total_rows)
    projection = projection.astype(jnp.bfloat16)
    image = (
        jnp.dot(standard, projection, preferred_element_type=jnp.float32) / math.sqrt(snps)
    ).astype(jnp.bfloat16)
    gram = jnp.einsum("rb,rc->bc", image, image, preferred_element_type=jnp.float32)
    cross = jnp.einsum("rs,rb->sb", standard, image, preferred_element_type=jnp.float32)
    gram, cross = everywhere((gram, cross))
    lower = jnp.linalg.cholesky(gram)
    basis = jax.scipy.linalg.solve_triangular(
        lower, image.astype(jnp.float32).T, lower=True
    ).T * math.sqrt(total_rows)
    scores = jax.scipy.linalg.solve_triangular(lower, cross.T, lower=True).T * math.sqrt(
        snps / total_rows
    )
    return (basis.astype(jnp.bfloat16), scores.astype(jnp.bfloat16))


def solution(mesh):
    finer = Mesh(mesh.devices.reshape(8, 2, 8, 4), ("rows_0", "rows_1", "cols_0", "cols_1"))
    in_specs = (P(ROWS_COLS, None), P(ROWS_COLS, None), P(ROWS_COLS))
    out_specs = (P(ROWS_COLS, None), P())
    return jax.shard_map(
        per_device, mesh=finer, in_specs=in_specs, out_specs=out_specs, check_vma=False
    )
```

profile of v0, /device:TPU:1, one launch (start us, length us, event | category | flops | bytes accessed | tf_op | source)
XLA Modules:
  0.0 322.4 jit_solution(6701976634498780750)
XLA Ops:
  0.7 4.3 %fusion.1 = (f32[2048]{0:T(1024)S(1)}, f32[2048]{0:T(1024)S(1)}, f32[2048]{0:T(1024)S(1)}) fusion(bf16[960,2048]{1,0:T(8,128)(2,1)} %param.3, s32[2048]{0:T(1024)S(1)} %add_select_fusion, s32[960]{0:T(1024)} %param.5), kind=kLoop, calls=%fused_computation.5 | loop fusion | flops 15722496 | bytes 3968768 | tf_op jit(solution)/shard_map/reduce_sum | solution.py:86
  5.0 0.3 reshape_reshape_reshape.22
  5.2 0.2 copy.7
  5.4 23.6 %all_to_all.100 = f32[64,8,12]{2,1,0:T(8,128)S(1)} all-to-all(f32[64,8,12]{2,1,0:T(8,128)S(1)} %copy.7), channel_id=1, replica_groups=mesh['rows_0'=8,'rows_1'=2,'cols_0'=8,'cols_1'=4] {'rows_1','cols_0','co..., dimensions={0} | all-to-all | bytes 49152 | tf_op jit(solution)/shard_map/all_to_all | solution.py:23
  29.1 16.4 %all_to_all.101 = f32[8,1,12]{2,1,0:T(1,128)S(1)} all-to-all(f32[8,1,12]{2,1,0:T(1,128)S(1)} %bitcast.65), channel_id=1, replica_groups=mesh['rows_0'=8,'rows_1'=2,'cols_0'=8,'cols_1'=4] {'rows_0'}, dimensions={0} | all-to-all | bytes 768 | tf_op jit(solution)/shard_map/all_to_all | solution.py:30
  45.5 8.9 %all_to_all.102 = f32[8,1,12]{2,1,0:T(1,128)S(1)} all-to-all(f32[8,1,12]{2,1,0:T(1,128)S(1)} %broadcast_in_dim.25), channel_id=1, replica_groups=mesh['rows_0'=8,'rows_1'=2,'cols_0'=8,'cols_1'=4] {'rows_0'}, dimensions={0} | all-to-all | bytes 768 | tf_op jit(solution)/shard_map/all_to_all | solution.py:42
  54.4 20.2 %all_to_all.103 = f32[64,8,12]{2,1,0:T(8,128)S(1)} all-to-all(f32[64,8,12]{2,1,0:T(8,128)S(1)} %broadcast_in_dim.27), channel_id=1, replica_groups=mesh['rows_0'=8,'rows_1'=2,'cols_0'=8,'cols_1'=4] {'rows_1','cols_0','co..., dimensions={0} | all-to-all | bytes 49152 | tf_op jit(solution)/shard_map/all_to_all | solution.py:42
  74.7 0.2 reshape_reshape_reshape.23
  75.0 3.3 %fusion.5 = bf16[960,2048]{1,0:T(8,128)(2,1)S(1)} fusion(bf16[960,2048]{1,0:T(8,128)(2,1)} %param.3, f32[2048]{0:T(1024)S(1)} %bitcast.62, f32[2048]{0:T(1024)S(1)} %bitcast.63, s32[2048]{0:T(1024)S(1)} %add_select_fusion, s32[960]{0:T(1024)S(1)} %copy-done.2), kind=kLoop, calls=%fused_computation.9 | loop fusion | flops 11796480 | bytes 7892736 | tf_op jit(solution)/shard_map/convert_element_type | solution.py:91
  78.2 1.9 copy-done.1
  80.1 1.3 fusion.18
  81.4 0.2 reshape_reshape_reshape.24
  81.6 0.6 copy.24
  82.2 33.7 %all_to_all.104 = f32[64,8,512]{2,1,0:T(8,128)S(1)} all-to-all(f32[64,8,512]{2,1,0:T(8,128)S(1)} %bitcast.52), channel_id=1, replica_groups=mesh['rows_0'=8,'rows_1'=2,'cols_0'=8,'cols_1'=4] {'rows_1','cols_0','co..., dimensions={0} | all-to-all | bytes 2097152 | tf_op jit(solution)/shard_map/all_to_all | solution.py:23
  116.0 9.0 %all_to_all.105 = f32[8,1,512]{2,1,0:T(1,128)S(1)} all-to-all(f32[8,1,512]{2,1,0:T(1,128)S(1)} %all_to_all.70), channel_id=1, replica_groups=mesh['rows_0'=8,'rows_1'=2,'cols_0'=8,'cols_1'=4] {'rows_0'}, dimensions={0} | all-to-all | bytes 32768 | tf_op jit(solution)/shard_map/all_to_all | solution.py:30
  125.1 9.0 %all_to_all.106 = f32[8,1,512]{2,1,0:T(1,128)S(1)} all-to-all(f32[8,1,512]{2,1,0:T(1,128)S(1)} %broadcast_in_dim.28), channel_id=1, replica_groups=mesh['rows_0'=8,'rows_1'=2,'cols_0'=8,'cols_1'=4] {'rows_0'}, dimensions={0} | all-to-all | bytes 32768 | tf_op jit(solution)/shard_map/all_to_all | solution.py:42
  134.1 0.1 broadcast_in_dim.30
  134.2 36.4 %all_to_all.107 = f32[64,8,512]{2,1,0:T(8,128)S(1)} all-to-all(f32[64,8,512]{2,1,0:T(8,128)S(1)} %broadcast_in_dim.30), channel_id=1, replica_groups=mesh['rows_0'=8,'rows_1'=2,'cols_0'=8,'cols_1'=4] {'rows_1','cols_0','co..., dimensions={0} | all-to-all | bytes 2097152 | tf_op jit(solution)/shard_map/all_to_all | solution.py:42
  170.6 0.1 fusion.9
  170.7 0.2 copy.11
  170.9 0.3 convert_element_type.34
  171.2 3.3 %fusion.8 = bf16[960,128]{1,0:T(8,128)(2,1)S(1)} fusion(bf16[960,2048]{1,0:T(8,128)(2,1)} %copy-done.1, bf16[2048,128]{1,0:T(8,128)(2,1)S(1)} %convert_element_type.34), kind=kOutput, calls=%fused_computation.15 | convolution fusion | flops 503562240 | bytes 4702208 | tf_op jit(solution)/shard_map/dot_general | solution.py:96
  174.5 0.3 fusion.19
  174.7 0.1 reshape_reshape_reshape.25
  174.9 0.2 copy.12
  175.0 0.8 reshape.74
  175.8 6.2 %all-to-all-start.8 = ((f32[64,1,256]{2,1,0:T(1,128)}), f32[64,1,256]{2,1,0:T(1,128)S(1)}, u32[]{:S(2)}, u32[]{:S(2)}) async-start(f32[64,1,256]{2,1,0:T(1,128)} %reshape.74), calls=%async_computation.8 | async-start | bytes 131072 | tf_op jit(solution)/shard_map/all_to_all | solution.py:23
  182.0 3.4 %fusion.20 = f32[2048,128]{1,0:T(8,128)S(1)} fusion(bf16[960,2048]{1,0:T(8,128)(2,1)} %copy-done.1, bf16[960,128]{1,0:T(8,128)(2,1)S(1)} %fusion.8), kind=kOutput, calls=%fused_computation.47 | convolution fusion | flops 503316480 | bytes 5226496 | tf_op jit(solution)/shard_map/rs,rb->sb/dot_general | solution.py:99
  185.4 0.2 reshape_reshape_reshape.27
  185.6 1.6 copy.23
  187.2 4.4 %all-to-all-done.8 = f32[64,1,256]{2,1,0:T(1,128)S(1)} async-done(((f32[64,1,256]{2,1,0:T(1,128)}), f32[64,1,256]{2,1,0:T(1,128)S(1)}, u32[]{:S(2)}, u32[]{:S(2)}) %all-to-all-start.8) | async-done | bytes 65568 | tf_op jit(solution)/shard_map/all_to_all | solution.py:23
  191.6 5.8 %all-to-all-start.12 = ((f32[64,8,512]{2,1,0:T(8,128)}), f32[64,8,512]{2,1,0:T(8,128)S(1)}, u32[]{:S(2)}, u32[]{:S(2)}) async-start(f32[64,8,512]{2,1,0:T(8,128)} %bitcast.47), calls=%async_computation.12 | async-start | bytes 2097152 | tf_op jit(solution)/shard_map/all_to_all | solution.py:23
  197.4 0.6 broadcast.141
  198.0 0.8 reduce.10
  198.8 0.1 reshape.75
  198.9 0.7 reduce_sum.106
  199.6 25.9 %all-to-all-done.12 = f32[64,8,512]{2,1,0:T(8,128)S(1)} async-done(((f32[64,8,512]{2,1,0:T(8,128)}), f32[64,8,512]{2,1,0:T(8,128)S(1)}, u32[]{:S(2)}, u32[]{:S(2)}) %all-to-all-start.12) | async-done | bytes 1048608 | tf_op jit(solution)/shard_map/all_to_all | solution.py:23
  225.5 3.3 %all-to-all-start.9 = ((f32[8,1,32]{2,1,0:T(1,128)}), f32[8,1,32]{2,1,0:T(1,128)S(1)}, u32[]{:S(2)}, u32[]{:S(2)}) async-start(f32[8,1,32]{2,1,0:T(1,128)} %bitcast.13), calls=%async_computation.9 | async-start | bytes 8192 | tf_op jit(solution)/shard_map/all_to_all | solution.py:30
  228.9 0.6 all_to_all.80
  229.5 5.7 %all-to-all-done.9 = f32[8,1,32]{2,1,0:T(1,128)S(1)} async-done(((f32[8,1,32]{2,1,0:T(1,128)}), f32[8,1,32]{2,1,0:T(1,128)S(1)}, u32[]{:S(2)}, u32[]{:S(2)}) %all-to-all-start.9) | async-done | bytes 1056 | tf_op jit(solution)/shard_map/all_to_all | solution.py:30
  235.2 3.3 %all-to-all-start.13 = ((f32[8,1,512]{2,1,0:T(1,128)}), f32[8,1,512]{2,1,0:T(1,128)S(1)}, u32[]{:S(2)}, u32[]{:S(2)}) async-start(f32[8,1,512]{2,1,0:T(1,128)} %all_to_all.80), calls=%async_computation.13 | async-start | bytes 32768 | tf_op jit(solution)/shard_map/all_to_all | solution.py:30
  238.6 6.5 %all-to-all-done.13 = f32[8,1,512]{2,1,0:T(1,128)S(1)} async-done(((f32[8,1,512]{2,1,0:T(1,128)}), f32[8,1,512]{2,1,0:T(1,128)S(1)}, u32[]{:S(2)}, u32[]{:S(2)}) %all-to-all-start.13) | async-done | bytes 16416 | tf_op jit(solution)/shard_map/all_to_all | solution.py:30
  245.1 0.6 broadcast_in_dim.31
  245.7 3.3 %all-to-all-start.10 = ((f32[8,1,32]{2,1,0:T(1,128)}), f32[8,1,32]{2,1,0:T(1,128)S(1)}, u32[]{:S(2)}, u32[]{:S(2)}) async-start(f32[8,1,32]{2,1,0:T(1,128)} %broadcast_in_dim.31), calls=%async_computation.10 | async-start | bytes 8192 | tf_op jit(solution)/shard_map/all_to_all | solution.py:42
  249.0 6.3 %all-to-all-done.10 = f32[8,1,32]{2,1,0:T(1,128)S(1)} async-done(((f32[8,1,32]{2,1,0:T(1,128)}), f32[8,1,32]{2,1,0:T(1,128)S(1)}, u32[]{:S(2)}, u32[]{:S(2)}) %all-to-all-start.10) | async-done | bytes 1056 | tf_op jit(solution)/shard_map/all_to_all | solution.py:42
  255.4 0.6 broadcast_in_dim.34
  256.0 3.3 %all-to-all-start.14 = ((f32[8,1,512]{2,1,0:T(1,128)}), f32[8,1,512]{2,1,0:T(1,128)S(1)}, u32[]{:S(2)}, u32[]{:S(2)}) async-start(f32[8,1,512]{2,1,0:T(1,128)} %broadcast_in_dim.34), calls=%async_computation.14 | async-start | bytes 32768 | tf_op jit(solution)/shard_map/all_to_all | solution.py:42
  259.4 0.8 reshape.76
  260.2 5.7 %all-to-all-done.14 = f32[8,1,512]{2,1,0:T(1,128)S(1)} async-done(((f32[8,1,512]{2,1,0:T(1,128)}), f32[8,1,512]{2,1,0:T(1,128)S(1)}, u32[]{:S(2)}, u32[]{:S(2)}) %all-to-all-start.14) | async-done | bytes 16416 | tf_op jit(solution)/shard_map/all_to_all | solution.py:42
  265.9 10.7 %all-to-all-start.11 = ((f32[64,1,256]{2,1,0:T(1,128)}), f32[64,1,256]{2,1,0:T(1,128)S(1)}, u32[]{:S(2)}, u32[]{:S(2)}) async-start(f32[64,1,256]{2,1,0:T(1,128)} %reshape.76), calls=%async_computation.11 | async-start | bytes 131072 | tf_op jit(solution)/shard_map/all_to_all | solution.py:42
  276.6 9.6 %all-to-all-done.11 = f32[64,1,256]{2,1,0:T(1,128)S(1)} async-done(((f32[64,1,256]{2,1,0:T(1,128)}), f32[64,1,256]{2,1,0:T(1,128)S(1)}, u32[]{:S(2)}, u32[]{:S(2)}) %all-to-all-start.11) | async-done | bytes 65568 | tf_op jit(solution)/shard_map/all_to_all | solution.py:42
  286.2 1.1 broadcast_in_dim.36
  287.3 4.5 %all-to-all-start.15 = ((f32[64,8,512]{2,1,0:T(8,128)}), f32[64,8,512]{2,1,0:T(8,128)S(1)}, u32[]{:S(2)}, u32[]{:S(2)}) async-start(f32[64,8,512]{2,1,0:T(8,128)} %broadcast_in_dim.36), calls=%async_computation.15 | async-start | bytes 2097152 | tf_op jit(solution)/shard_map/all_to_all | solution.py:42
  291.8 0.8 reduce.11
  292.7 0.1 reshape.77
  292.9 0.1 reshape_reshape_reshape.26
  293.1 11.7 %cholesky.16 = f32[128,128]{1,0:T(8,128)S(1)} custom-call(f32[128,128]{1,0:T(8,128)S(1)} %fusion.13), custom_call_target="Cholesky" | custom-call | tf_op jit(solution)/shard_map/jit(cholesky)/cholesky | solution.py:101
  304.8 0.6 compare_reduce_fusion
  305.5 0.7 fusion.10
  306.1 9.8 %custom-call.10 = f32[1,128,128]{1,2,0:T(8,128)S(1)} custom-call(f32[1,128,128]{2,1,0:T(8,128)S(1)} %fusion.10), custom_call_target="InvertDiagBlocksLowerTriangular" | custom-call | tf_op jit(solution)/shard_map/jit(_solve_triangular)/triangular_solve | solution.py:102
  316.0 1.1 fusion.7
  317.0 2.9 all-to-all-done.15
  319.9 0.6 copy.16
  320.6 1.8 fusion.6
  (28 shorter events, 0.9 us)
Async XLA Ops:
  0.6 79.5 %copy-start = (bf16[960,128]{1,0:T(8,128)(2,1)S(1)}, bf16[960,128]{1,0:T(8,128)(2,1)}, u32[]{:S(2)}) copy-start(bf16[960,128]{1,0:T(8,128)(2,1)} %param.4) | copy-start | bytes 737284
  0.6 74.3 %copy-start.2 = (s32[960]{0:T(1024)S(1)}, s32[960]{0:T(1024)}, u32[]{:S(2)}) copy-start(s32[960]{0:T(1024)} %param.5) | copy-start | bytes 11524
  78.2 1.9 copy-start.1
  175.8 15.7 %all-to-all-start.8 = ((f32[64,1,256]{2,1,0:T(1,128)}), f32[64,1,256]{2,1,0:T(1,128)S(1)}, u32[]{:S(2)}, u32[]{:S(2)}) async-start(f32[64,1,256]{2,1,0:T(1,128)} %reshape.74), calls=%async_computation.8 | async-start | bytes 131072 | tf_op jit(solution)/shard_map/all_to_all | solution.py:23
  191.6 33.9 %all-to-all-start.12 = ((f32[64,8,512]{2,1,0:T(8,128)}), f32[64,8,512]{2,1,0:T(8,128)S(1)}, u32[]{:S(2)}, u32[]{:S(2)}) async-start(f32[64,8,512]{2,1,0:T(8,128)} %bitcast.47), calls=%async_computation.12 | async-start | bytes 2097152 | tf_op jit(solution)/shard_map/all_to_all | solution.py:23
  225.5 9.7 %all-to-all-start.9 = ((f32[8,1,32]{2,1,0:T(1,128)}), f32[8,1,32]{2,1,0:T(1,128)S(1)}, u32[]{:S(2)}, u32[]{:S(2)}) async-start(f32[8,1,32]{2,1,0:T(1,128)} %bitcast.13), calls=%async_computation.9 | async-start | bytes 8192 | tf_op jit(solution)/shard_map/all_to_all | solution.py:30
  235.2 9.9 %all-to-all-start.13 = ((f32[8,1,512]{2,1,0:T(1,128)}), f32[8,1,512]{2,1,0:T(1,128)S(1)}, u32[]{:S(2)}, u32[]{:S(2)}) async-start(f32[8,1,512]{2,1,0:T(1,128)} %all_to_all.80), calls=%async_computation.13 | async-start | bytes 32768 | tf_op jit(solution)/shard_map/all_to_all | solution.py:30
  245.7 9.7 %all-to-all-start.10 = ((f32[8,1,32]{2,1,0:T(1,128)}), f32[8,1,32]{2,1,0:T(1,128)S(1)}, u32[]{:S(2)}, u32[]{:S(2)}) async-start(f32[8,1,32]{2,1,0:T(1,128)} %broadcast_in_dim.31), calls=%async_computation.10 | async-start | bytes 8192 | tf_op jit(solution)/shard_map/all_to_all | solution.py:42
  256.0 9.9 %all-to-all-start.14 = ((f32[8,1,512]{2,1,0:T(1,128)}), f32[8,1,512]{2,1,0:T(1,128)S(1)}, u32[]{:S(2)}, u32[]{:S(2)}) async-start(f32[8,1,512]{2,1,0:T(1,128)} %broadcast_in_dim.34), calls=%async_computation.14 | async-start | bytes 32768 | tf_op jit(solution)/shard_map/all_to_all | solution.py:42
  265.9 20.3 %all-to-all-start.11 = ((f32[64,1,256]{2,1,0:T(1,128)}), f32[64,1,256]{2,1,0:T(1,128)S(1)}, u32[]{:S(2)}, u32[]{:S(2)}) async-start(f32[64,1,256]{2,1,0:T(1,128)} %reshape.76), calls=%async_computation.11 | async-start | bytes 131072 | tf_op jit(solution)/shard_map/all_to_all | solution.py:42
  287.3 32.6 %all-to-all-start.15 = ((f32[64,8,512]{2,1,0:T(8,128)}), f32[64,8,512]{2,1,0:T(8,128)S(1)}, u32[]{:S(2)}, u32[]{:S(2)}) async-start(f32[64,8,512]{2,1,0:T(8,128)} %broadcast_in_dim.36), calls=%async_computation.15 | async-start | bytes 2097152 | tf_op jit(solution)/shard_map/all_to_all | solution.py:42
where the time goes:
time: 323 us; the launch traced here: 322 us
  blocking collectives  157 us (49%)
  waiting for transfers between devices  67 us (21%)
  starting transfers between devices  40.5 us (13%)
  other arithmetic  33.3 us (10%)
  local copies, waits for them, and re-layouts  12.3 us (4%)
  matrix products  11.1 us (3%)
    all_to_all x4, blocking collectives, sent_to_all(): lax.all_to_all(jnp.broadcast_to(array[None], (size, *array.shape)), axis,...  74.5 us
    all_to_all x2, blocking collectives, sum_at_owner(): lax.all_to_all(blocks, axis, split_axis=0, concat_axis=0, tiled=True)  57.3 us
    all_to_all x2, waiting for transfers between devices, sum_at_owner(): lax.all_to_all(blocks, axis, split_axis=0, concat_axis=0, tiled=True)  30.3 us
    all_to_all x2, blocking collectives, summed_rows(): return jnp.sum(lax.all_to_all(own, far, 0, 0, tiled=True), axis=0)  25.3 us
    all_to_all x4, waiting for transfers between devices, sent_to_all(): lax.all_to_all(jnp.broadcast_to(array[None], (size, *array.shape)), axis,...  24.5 us
    all_to_all x4, starting transfers between devices, sent_to_all(): lax.all_to_all(jnp.broadcast_to(array[None], (size, *array.shape)), axis,...  21.9 us
    another operation x3, other arithmetic, per_device(): lower = jnp.linalg.cholesky(gram)  12.4 us
    all_to_all x2, waiting for transfers between devices, summed_rows(): return jnp.sum(lax.all_to_all(own, far, 0, 0, tiled=True), axis=0)  12.2 us
  transfers between devices with their start and end apart: 8, of which 8 were waited for; matrix products, arithmetic and copies ran while one was open for 10% of the time, Pallas kernels for 0%

commit v1 on v0

v1 whole, which is shorter than its diff:
```python
import math

import jax
import jax.numpy as jnp
from jax import lax
from jax.sharding import Mesh
from jax.sharding import PartitionSpec as P

BLOCK_SNPS = 128
ALL = ("z", "c", "y", "x")
SWAP = ((0, 1), (1, 0))


def exchanged(blocks, axis):
    return lax.all_to_all(blocks, axis, 0, 0, tiled=True)


def summed_parts(array, axis):
    size = lax.axis_size(axis)
    blocks = array.reshape(size, array.shape[0] // size, array.shape[1])
    return jnp.sum(exchanged(blocks, axis), 0)


def copies(array, axis):
    return exchanged(jnp.broadcast_to(array[None], (lax.axis_size(axis), *array.shape)), axis)


def swapped(array):
    return lax.ppermute(array, "c", SWAP)


def per_device(genotypes, probes, missing_codes):
    rows, snps = genotypes.shape
    probe_count = probes.shape[1]
    total_rows = rows * math.prod(lax.axis_size(a) for a in ALL)
    core = lax.axis_index("c")
    blocks = snps // BLOCK_SNPS
    half = snps // 2
    block_half = blocks // 2
    wide_x, wide_y = lax.axis_size("x"), lax.axis_size("y")

    snp_block = jnp.arange(snps) // BLOCK_SNPS
    seen = snp_block[None, :] != missing_codes[:, None]
    observed = seen.astype(jnp.float32)
    kept = jnp.where(seen, genotypes, jnp.zeros_like(genotypes))
    dosage = kept.astype(jnp.float32)
    raw = jnp.einsum("rs,rb->sb", kept, probes, preferred_element_type=jnp.float32)
    total = jnp.sum(dosage, 0).reshape(blocks, BLOCK_SNPS)
    square = jnp.sum(dosage * dosage, 0).reshape(blocks, BLOCK_SNPS)
    by_block = jnp.arange(blocks)[None, :] != missing_codes[:, None]
    seen_probes = jnp.einsum(
        "rk,rb->kb", by_block.astype(jnp.bfloat16), probes, preferred_element_type=jnp.float32
    )
    count = jnp.broadcast_to(
        jnp.sum(by_block.astype(jnp.float32), 0)[:, None], (blocks, BLOCK_SNPS)
    )

    def part(which):
        def take(a):
            n = a.shape[0] // 2
            return lax.dynamic_slice_in_dim(a, which * n, n)

        return jnp.concatenate([take(a) for a in (raw, total, square, seen_probes, count)])

    mine = part(core) + swapped(part(1 - core))
    mine = summed_parts(mine, "x")
    mine = summed_parts(mine, "y")
    mine = jnp.sum(copies(mine, "z"), 0)
    mine = copies(mine, "y").reshape(-1, probe_count)
    mine = copies(mine, "x").reshape(-1, probe_count)
    other = swapped(mine)
    first = jnp.where(core == 0, mine, other)
    second = jnp.where(core == 0, other, mine)

    def joined(start, length):
        return jnp.concatenate([first[start : start + length], second[start : start + length]])

    raw = joined(0, half)
    total, square, seen_probes, count = (
        joined(half + i * block_half, block_half) for i in range(4)
    )
    counted = jnp.maximum(count, 1.0)
    mean = total / counted
    inv_sd = 1.0 / jnp.sqrt(square / counted - mean * mean + 1e-05)
    centred = (
        raw.reshape(blocks, BLOCK_SNPS, probe_count) - mean[:, :, None] * seen_probes[:, None, :]
    )
    projection = (centred * inv_sd[:, :, None] / math.sqrt(total_rows)).astype(jnp.bfloat16)
    projection = projection.reshape(snps, probe_count)
    standard = (
        (genotypes.astype(jnp.float32) - mean.reshape(1, snps)) * inv_sd.reshape(1, snps) * observed
    ).astype(jnp.bfloat16)
    image = (
        jnp.dot(standard, projection, preferred_element_type=jnp.float32) / math.sqrt(snps)
    ).astype(jnp.bfloat16)
    gram = jnp.einsum("rb,rc->bc", image, image, preferred_element_type=jnp.float32)
    cross = jnp.einsum("rs,rb->sb", standard, image, preferred_element_type=jnp.float32)

    def halves(which):
        n = probe_count // 2
        return jnp.concatenate(
            [
                lax.dynamic_slice_in_dim(cross, which * half, half),
                lax.dynamic_slice_in_dim(gram, which * n, n),
            ]
        )

    mine = halves(core) + swapped(halves(1 - core))
    over_x = jnp.concatenate(
        [
            mine[:half].reshape(wide_x, half // wide_x, probe_count),
            jnp.broadcast_to(mine[None, half:], (wide_x, probe_count // 2, probe_count)),
        ],
        1,
    )
    mine = jnp.sum(exchanged(over_x, "x"), 0)
    shard = half // wide_x
    over_y = jnp.concatenate(
        [
            mine[:shard].reshape(wide_y, shard // wide_y, probe_count),
            mine[shard:].reshape(wide_y, probe_count // 2 // wide_y, probe_count),
        ],
        1,
    )
    mine = jnp.sum(exchanged(over_y, "y"), 0)
    mine = jnp.sum(copies(mine, "z"), 0)
    back = copies(mine, "y")
    shard_y = shard // wide_y
    gram_half = back[:, shard_y:].reshape(probe_count // 2, probe_count)
    cross_half = copies(back[:, :shard_y].reshape(shard, probe_count), "x").reshape(
        half, probe_count
    )
    gram_other = swapped(gram_half)
    gram = jnp.where(
        core == 0,
        jnp.concatenate([gram_half, gram_other]),
        jnp.concatenate([gram_other, gram_half]),
    )
    lower = jnp.linalg.cholesky(gram)
    inverse = jax.scipy.linalg.solve_triangular(
        lower, jnp.eye(probe_count, dtype=jnp.float32), lower=True
    )
    basis = jnp.dot(image.astype(jnp.float32), inverse.T, precision=lax.Precision.HIGHEST)
    cross_other = swapped(cross_half)
    cross = jnp.where(
        core == 0,
        jnp.concatenate([cross_half, cross_other]),
        jnp.concatenate([cross_other, cross_half]),
    )
    scores = jnp.dot(cross, inverse.T, precision=lax.Precision.HIGHEST)
    return (
        (basis * math.sqrt(total_rows)).astype(jnp.bfloat16),
        (scores * math.sqrt(snps / total_rows)).astype(jnp.bfloat16),
    )


def solution(mesh):
    finer = Mesh(mesh.devices.reshape(8, 2, 8, 4), ALL)
    spec = (P(ALL, None), P(ALL, None), P(ALL))
    return jax.shard_map(
        per_device, mesh=finer, in_specs=spec, out_specs=(P(ALL, None), P()), check_vma=False
    )
```

time: 323 us -> 183 us (0.57)
  waiting for transfers between devices: 67 us -> 4.56 us
  blocking collectives: 157 us -> 106 us
  local copies, waits for them, and re-layouts: 12.3 us -> 1.71 us
  starting transfers between devices: 40.5 us -> 31.8 us
  other arithmetic: 33.3 us -> 28.3 us
    all_to_all x8 -> x1, waiting for transfers between devices: 67 us -> 0.01 us  [exchanged(): return lax.all_to_all(blocks, axis, 0, 0, tiled=True)]
    all_to_all x8 -> x9, blocking collectives: 157 us -> 106 us  [exchanged(): return lax.all_to_all(blocks, axis, 0, 0, tiled=True)]
    all_to_all x8 -> x1, starting transfers between devices: 40.5 us -> 3.65 us  [exchanged(): return lax.all_to_all(blocks, axis, 0, 0, tiled=True)]
    ppermute x0 -> x5, starting transfers between devices: none -> 28.1 us  [swapped(): return lax.ppermute(array, 'c', SWAP)]
    ppermute x0 -> x5, waiting for transfers between devices: none -> 4.56 us  [swapped(): return lax.ppermute(array, 'c', SWAP)]
    unnamed x12, local copies, waits for them, and re-layouts: 3.69 us -> 0.11 us
    another operation x10 -> x0, local copies, waits for them, and re-layouts: 3.38 us -> none  [the longest x6 2.92 us: split_up(): array.reshape(*lengths[:dim], size, lengths[dim] // size, *lengths[dim +...]
    dot_general x1 -> x4, matrix products: 1.32 us -> 4.63 us  [the longest x1 1.78 us: per_device(): scores = jnp.dot(cross, inverse.T, precision=lax.Precision.HIGHEST)]
  transfers between devices with their start and end apart: 8 -> 6, of which waited for: 8 -> 3; matrix products, arithmetic and copies ran while one was open for 10% -> 14% of each run, Pallas kernels for 0% -> 0%
where the time goes in v1:
time: 183 us; the launch traced here: 182 us
  blocking collectives  106 us (58%)
  starting transfers between devices  31.8 us (17%)
  other arithmetic  28.3 us (15%)
  matrix products  8.78 us (5%)
  waiting for transfers between devices  4.56 us (2%)
    all_to_all x9, blocking collectives, exchanged(): return lax.all_to_all(blocks, axis, 0, 0, tiled=True)  106 us
    ppermute x5, starting transfers between devices, swapped(): return lax.ppermute(array, 'c', SWAP)  28.1 us
    another operation x3, other arithmetic, per_device(): lower = jnp.linalg.cholesky(gram)  12.4 us
    another operation x2, other arithmetic, per_device(): jax.scipy.linalg.solve_triangular(lower, jnp.eye(probe_count, dtype=jnp.f...  10.5 us
    ppermute x5, waiting for transfers between devices, swapped(): return lax.ppermute(array, 'c', SWAP)  4.56 us
    reduce_sum x1, other arithmetic, per_device(): square = jnp.sum(dosage * dosage, 0).reshape(blocks, BLOCK_SNPS)  3.69 us
  transfers between devices with their start and end apart: 6, of which 3 were waited for; matrix products, arithmetic and copies ran while one was open for 14% of the time, Pallas kernels for 0%

profile of v1, /device:TPU:1, one launch (start us, length us, event | category | flops | bytes accessed | tf_op | source)
XLA Modules:
  0.0 182.0 jit_solution(1802942768719678179)
XLA Ops:
  0.6 0.0 copy-start
  0.6 0.0 copy-start.3
  0.7 0.0 copy-start.1
  0.7 3.7 %fusion = (f32[2048]{0:T(1024)S(1)}, f32[2048]{0:T(1024)S(1)}) fusion(bf16[960,2048]{1,0:T(8,128)(2,1)} %param.3, s32[960]{0:T(1024)} %param.5, s32[2048]{0:T(1024)S(1)} %add_select_fusion), kind=kLoop, calls=%fused_computation.4 | loop fusion | flops 11792384 | bytes 3960576 | tf_op jit(solution)/shard_map/reduce_sum | solution.py:49
  4.4 0.0 copy-done
  4.4 0.0 copy-done.3
  4.4 0.0 copy-done.1
  4.4 1.6 fusion.39
  6.0 0.2 fusion.21
  6.2 0.1 convert_reduce_fusion.1
  6.3 0.1 dynamic-slice_dynamic-update-slice_fusion
  6.4 0.1 fusion.42
  6.5 0.1 constant_dynamic-update-slice_fusion.4
  6.6 8.8 %collective-permute-start = (f32[1056,128]{1,0:T(8,128)S(1)}, f32[1056,128]{1,0:T(8,128)S(1)}, u32[]{:S(2)}, u32[]{:S(2)}) collective-permute-start(f32[1056,128]{1,0:T(8,128)S(1)} %constant_dynamic-update-slice_fusion.4), channel_id=1, source_target_pairs={{0,32},{32,0},{1,33},{33,1},{2,34},{34,2},{3,35},{35,3},{4,36},{36... | collective-permute-start | bytes 1622024 | tf_op jit(solution)/shard_map/ppermute | solution.py:29
  15.4 0.1 constant_dynamic-update-slice_fusion
  15.4 1.5 collective-permute-done
  16.9 0.1 add.69
  17.0 11.8 %all_to_all.50 = f32[4,264,128]{2,1,0:T(8,128)S(1)} all-to-all(f32[4,264,128]{2,1,0:T(8,128)S(1)} %bitcast.72), channel_id=1, replica_groups=mesh['z'=8,'c'=2,'y'=8,'x'=4] {'x'}, dimensions={0} | all-to-all | bytes 1081344 | tf_op jit(solution)/shard_map/all_to_all | solution.py:15
  28.8 10.7 %all_to_all.51 = f32[8,33,128]{2,1,0:T(8,128)S(1)} all-to-all(f32[8,33,128]{2,1,0:T(8,128)S(1)} %reshape.163), channel_id=1, replica_groups=mesh['z'=8,'c'=2,'y'=8,'x'=4] {'y'}, dimensions={0} | all-to-all | bytes 270336 | tf_op jit(solution)/shard_map/all_to_all | solution.py:15
  39.5 18.2 %all_to_all.52 = f32[8,33,128]{2,1,0:T(8,128)S(1)} all-to-all(f32[8,33,128]{2,1,0:T(8,128)S(1)} %broadcast_in_dim.28), channel_id=1, replica_groups=mesh['z'=8,'c'=2,'y'=8,'x'=4] {'z'}, dimensions={0} | all-to-all | bytes 270336 | tf_op jit(solution)/shard_map/all_to_all | solution.py:15
  57.8 10.7 %all_to_all.53 = f32[8,33,128]{2,1,0:T(8,128)S(1)} all-to-all(f32[8,33,128]{2,1,0:T(8,128)S(1)} %broadcast_in_dim.29), channel_id=1, replica_groups=mesh['z'=8,'c'=2,'y'=8,'x'=4] {'y'}, dimensions={0} | all-to-all | bytes 270336 | tf_op jit(solution)/shard_map/all_to_all | solution.py:15
  68.5 9.4 %all_to_all.54 = f32[4,264,128]{2,1,0:T(8,128)S(1)} all-to-all(f32[4,264,128]{2,1,0:T(8,128)S(1)} %broadcast_in_dim.31), channel_id=1, replica_groups=mesh['z'=8,'c'=2,'y'=8,'x'=4] {'x'}, dimensions={0} | all-to-all | bytes 1081344 | tf_op jit(solution)/shard_map/all_to_all | solution.py:15
  77.9 8.5 %collective-permute-start.1 = (f32[1056,128]{1,0:T(8,128)S(1)}, f32[1056,128]{1,0:T(8,128)S(1)}, u32[]{:S(2)}, u32[]{:S(2)}) collective-permute-start(f32[1056,128]{1,0:T(8,128)S(1)} %bitcast.73), channel_id=1, source_target_pairs={{0,32},{32,0},{1,33},{33,1},{2,34},{34,2},{3,35},{35,3},{4,36},{36... | collective-permute-start | bytes 1622024 | tf_op jit(solution)/shard_map/ppermute | solution.py:29
  86.3 0.0 copy-start.2
  86.4 1.5 collective-permute-done.1
  87.9 0.1 broadcast_select_fusion.1
  88.1 1.1 fusion.7
  89.2 0.0 copy-done.2
  89.2 1.7 fusion.4
  91.0 1.9 %fusion.14 = f32[2048,128]{1,0:T(8,128)S(1)} fusion(bf16[960,128]{1,0:T(8,128)(2,1)S(1)} %fusion.4, bf16[960,2048]{1,0:T(8,128)(2,1)S(1)} %copy-done.2, f32[2048]{0:T(1024)S(1)} %fusion.29, f32[2048]{0:T(1024)S(1)} %fusion.25, s32[2048]{0:T(1024)S(1)} %add_select_fusion, s32[960]{0:T(1024)S(1)} %copy-done.3), kind=kOutput, calls=%fused_computation.31 | convolution fusion | flops 515112960 | bytes 5254912 | tf_op jit(solution)/shard_map/rs,rb->sb/dot_general | solution.py:97
  92.9 0.3 fusion.43
  93.1 0.1 constant_dynamic-slice_fusion.3
  93.3 2.3 %collective-permute-start.2 = (f32[1088,128]{1,0:T(8,128)S(1)}, f32[1088,128]{1,0:T(8,128)S(1)}, u32[]{:S(2)}, u32[]{:S(2)}) collective-permute-start(f32[1088,128]{1,0:T(8,128)S(1)} %pad_maximum_fusion.1), channel_id=1, source_target_pairs={{0,32},{32,0},{1,33},{33,1},{2,34},{34,2},{3,35},{35,3},{4,36},{36... | collective-permute-start | bytes 1671176 | tf_op jit(solution)/shard_map/ppermute | solution.py:29
  95.6 1.6 collective-permute-done.2
  97.2 0.1 maximum_add_fusion
  97.3 13.0 %all_to_all.55 = f32[4,320,128]{2,1,0:T(8,128)S(1)} all-to-all(f32[4,320,128]{2,1,0:T(8,128)S(1)} %pad_maximum_fusion), channel_id=1, replica_groups=mesh['z'=8,'c'=2,'y'=8,'x'=4] {'x'}, dimensions={0} | all-to-all | bytes 1310720 | tf_op jit(solution)/shard_map/all_to_all | solution.py:15
  110.5 10.5 %all_to_all.56 = f32[8,40,128]{2,1,0:T(8,128)S(1)} all-to-all(f32[8,40,128]{2,1,0:T(8,128)S(1)} %pad_maximum_fusion.2), channel_id=1, replica_groups=mesh['z'=8,'c'=2,'y'=8,'x'=4] {'y'}, dimensions={0} | all-to-all | bytes 327680 | tf_op jit(solution)/shard_map/all_to_all | solution.py:15
  121.0 10.8 %all_to_all.57 = f32[8,40,128]{2,1,0:T(8,128)S(1)} all-to-all(f32[8,40,128]{2,1,0:T(8,128)S(1)} %broadcast_in_dim.33), channel_id=1, replica_groups=mesh['z'=8,'c'=2,'y'=8,'x'=4] {'z'}, dimensions={0} | all-to-all | bytes 327680 | tf_op jit(solution)/shard_map/all_to_all | solution.py:15
  131.8 10.8 %all_to_all.58 = f32[8,40,128]{2,1,0:T(8,128)S(1)} all-to-all(f32[8,40,128]{2,1,0:T(8,128)S(1)} %broadcast_in_dim.34), channel_id=1, replica_groups=mesh['z'=8,'c'=2,'y'=8,'x'=4] {'y'}, dimensions={0} | all-to-all | bytes 327680 | tf_op jit(solution)/shard_map/all_to_all | solution.py:15
  142.5 0.1 copy.17
  142.6 6.7 %collective-permute-start.3 = (f32[64,128]{0,1:T(8,128)S(1)}, f32[64,128]{0,1:T(8,128)S(1)}, u32[]{:S(2)}, u32[]{:S(2)}) collective-permute-start(f32[64,128]{0,1:T(8,128)S(1)} %copy.17), channel_id=1, source_target_pairs={{0,32},{32,0},{1,33},{33,1},{2,34},{34,2},{3,35},{35,3},{4,36},{36... | collective-permute-start | bytes 98312 | tf_op jit(solution)/shard_map/ppermute | solution.py:29
  149.3 0.8 broadcast_in_dim.36
  150.2 3.7 %all-to-all-start.9 = ((f32[4,256,128]{2,1,0:T(8,128)}), f32[4,256,128]{2,1,0:T(8,128)S(1)}, u32[]{:S(2)}, u32[]{:S(2)}) async-start(f32[4,256,128]{2,1,0:T(8,128)} %broadcast_in_dim.36), calls=%async_computation.9 | async-start | bytes 1048576 | tf_op jit(solution)/shard_map/all_to_all | solution.py:15
  153.8 0.0 collective-permute-done.3
  153.8 0.1 maximum_select_fusion.2
  153.9 0.1 copy.19
  154.1 11.7 %cholesky.17 = f32[128,128]{1,0:T(8,128)S(1)} custom-call(f32[128,128]{1,0:T(8,128)S(1)} %fusion.20), custom_call_target="Cholesky" | custom-call | tf_op jit(solution)/shard_map/jit(cholesky)/cholesky | solution.py:139
  165.8 0.6 compare_reduce_fusion
  166.5 0.0 all-to-all-done.9
  166.5 1.9 %collective-permute-start.4 = (f32[1024,128]{1,0:T(8,128)S(1)}, f32[1024,128]{1,0:T(8,128)S(1)}, u32[]{:S(2)}, u32[]{:S(2)}) collective-permute-start(f32[1024,128]{1,0:T(8,128)S(1)} %bitcast.76), channel_id=1, source_target_pairs={{0,32},{32,0},{1,33},{33,1},{2,34},{34,2},{3,35},{35,3},{4,36},{36... | collective-permute-start | bytes 1572872 | tf_op jit(solution)/shard_map/ppermute | solution.py:29
  168.4 0.7 fusion.17
  169.0 9.8 %custom-call.7 = f32[1,128,128]{1,2,0:T(8,128)S(1)} custom-call(f32[1,128,128]{2,1,0:T(8,128)S(1)} %fusion.17), custom_call_target="InvertDiagBlocksLowerTriangular" | custom-call | tf_op jit(solution)/shard_map/jit(_solve_triangular)/triangular_solve | solution.py:140
  178.9 0.2 fusion.18
  179.1 1.1 fusion.3
  180.2 0.0 collective-permute-done.4
  180.2 1.8 fusion.2
  (38 shorter events, 0.6 us)
Async XLA Ops:
  0.6 3.8 %copy-start = (bf16[960,128]{1,0:T(8,128)(2,1)S(1)}, bf16[960,128]{1,0:T(8,128)(2,1)}, u32[]{:S(2)}) copy-start(bf16[960,128]{1,0:T(8,128)(2,1)} %param.4) | copy-start | bytes 737284
  0.6 3.8 %copy-start.3 = (s32[960]{0:T(1024)S(1)}, s32[960]{0:T(1024)}, u32[]{:S(2)}) copy-start(s32[960]{0:T(1024)} %param.5) | copy-start | bytes 11524
  0.7 3.7 %copy-start.1 = (bf16[960,2048]{1,0:T(8,128)(2,1)S(1)}, bf16[960,2048]{1,0:T(8,128)(2,1)}, u32[]{:S(2)}) copy-start(bf16[960,2048]{1,0:T(8,128)(2,1)} %param.3) | copy-start | bytes 11796484
  6.6 10.3 %collective-permute-start = (f32[1056,128]{1,0:T(8,128)S(1)}, f32[1056,128]{1,0:T(8,128)S(1)}, u32[]{:S(2)}, u32[]{:S(2)}) collective-permute-start(f32[1056,128]{1,0:T(8,128)S(1)} %constant_dynamic-update-slice_fusion.4), channel_id=1, source_target_pairs={{0,32},{32,0},{1,33},{33,1},{2,34},{34,2},{3,35},{35,3},{4,36},{36... | collective-permute-start | bytes 1622024 | tf_op jit(solution)/shard_map/ppermute | solution.py:29
  77.9 10.0 %collective-permute-start.1 = (f32[1056,128]{1,0:T(8,128)S(1)}, f32[1056,128]{1,0:T(8,128)S(1)}, u32[]{:S(2)}, u32[]{:S(2)}) collective-permute-start(f32[1056,128]{1,0:T(8,128)S(1)} %bitcast.73), channel_id=1, source_target_pairs={{0,32},{32,0},{1,33},{33,1},{2,34},{34,2},{3,35},{35,3},{4,36},{36... | collective-permute-start | bytes 1622024 | tf_op jit(solution)/shard_map/ppermute | solution.py:29
  86.3 2.9 %copy-start.2 = (bf16[960,2048]{1,0:T(8,128)(2,1)S(1)}, bf16[960,2048]{1,0:T(8,128)(2,1)}, u32[]{:S(2)}) copy-start(bf16[960,2048]{1,0:T(8,128)(2,1)} %param.3) | copy-start | bytes 11796484
  93.3 3.9 %collective-permute-start.2 = (f32[1088,128]{1,0:T(8,128)S(1)}, f32[1088,128]{1,0:T(8,128)S(1)}, u32[]{:S(2)}, u32[]{:S(2)}) collective-permute-start(f32[1088,128]{1,0:T(8,128)S(1)} %pad_maximum_fusion.1), channel_id=1, source_target_pairs={{0,32},{32,0},{1,33},{33,1},{2,34},{34,2},{3,35},{35,3},{4,36},{36... | collective-permute-start | bytes 1671176 | tf_op jit(solution)/shard_map/ppermute | solution.py:29
  142.6 11.2 %collective-permute-start.3 = (f32[64,128]{0,1:T(8,128)S(1)}, f32[64,128]{0,1:T(8,128)S(1)}, u32[]{:S(2)}, u32[]{:S(2)}) collective-permute-start(f32[64,128]{0,1:T(8,128)S(1)} %copy.17), channel_id=1, source_target_pairs={{0,32},{32,0},{1,33},{33,1},{2,34},{34,2},{3,35},{35,3},{4,36},{36... | collective-permute-start | bytes 98312 | tf_op jit(solution)/shard_map/ppermute | solution.py:29
  150.2 16.3 %all-to-all-start.9 = ((f32[4,256,128]{2,1,0:T(8,128)}), f32[4,256,128]{2,1,0:T(8,128)S(1)}, u32[]{:S(2)}, u32[]{:S(2)}) async-start(f32[4,256,128]{2,1,0:T(8,128)} %broadcast_in_dim.36), calls=%async_computation.9 | async-start | bytes 1048576 | tf_op jit(solution)/shard_map/all_to_all | solution.py:15
  166.5 13.7 %collective-permute-start.4 = (f32[1024,128]{1,0:T(8,128)S(1)}, f32[1024,128]{1,0:T(8,128)S(1)}, u32[]{:S(2)}, u32[]{:S(2)}) collective-permute-start(f32[1024,128]{1,0:T(8,128)S(1)} %bitcast.76), channel_id=1, source_target_pairs={{0,32},{32,0},{1,33},{33,1},{2,34},{34,2},{3,35},{35,3},{4,36},{36... | collective-permute-start | bytes 1572872 | tf_op jit(solution)/shard_map/ppermute | solution.py:29

commit v2 on v1

--- a/solution.py
+++ b/solution.py
@@ -3,6 +3,8 @@
 import jax
 import jax.numpy as jnp
 from jax import lax
+from jax.experimental import pallas as pl
+from jax.experimental.pallas import tpu as pltpu
 from jax.sharding import Mesh
 from jax.sharding import PartitionSpec as P
 
@@ -27,6 +29,92 @@
 
 def swapped(array):
     return lax.ppermute(array, "c", SWAP)
+
+def inverse_factor(gram):
+    n = gram.shape[0]
+    step = 8
+    left = gram
+    inv = (
+        lax.broadcasted_iota(jnp.int32, (n, n), 0) == lax.broadcasted_iota(jnp.int32, (n, n), 1)
+    ).astype(jnp.float32)
+    row_of = lax.broadcasted_iota(jnp.int32, (step, n), 0)
+    done = []
+    for base in range(0, n, step):
+        upper = left[:step]
+        under = inv[:step]
+        a = [
+            [
+                jnp.broadcast_to(upper[i : i + 1, base + k : base + k + 1], (step, n))
+                if k >= i
+                else None
+                for k in range(step)
+            ]
+            for i in range(step)
+        ]
+        x = [[None] * step for _ in range(step)]
+        scale = []
+        for t in range(step):
+            r = lax.rsqrt(a[t][t])
+            scale.append(r)
+            u = [None] * step
+            for k in range(t + 1, step):
+                u[k] = a[t][k] * r
+            for i in range(t + 1, step):
+                for k in range(i, step):
+                    a[i][k] = a[i][k] - u[i] * u[k]
+            a[t] = u
+        for i in range(step):
+            x[i][i] = scale[i]
+            for k in range(i):
+                s = a[k][i] * x[k][k]
+                for m in range(k + 1, i):
+                    s = s + a[m][i] * x[m][k]
+                x[i][k] = -s * scale[i]
+        cols = []
+        for k in range(step):
+            col = jnp.zeros((step, n), jnp.float32)
+            for i in range(k, step):
+                col = jnp.where(row_of == i, x[i][k], col)
+            cols.append(col)
+        both = jnp.concatenate([upper, under], 1)
+        out = sum(
+            jnp.concatenate([cols[k], cols[k]], 1) * both[k : k + 1] for k in range(step)
+        )
+        done.append(out[:, n:])
+        if base + step < n:
+            u = out[:, :n]
+            prod = lax.dot_general(
+                u, out, (((0,), (0,)), ((), ())), precision=lax.Precision.HIGHEST, preferred_element_type=jnp.float32
+            )
+            left = left[step:] - prod[base + step :, :n]
+            inv = inv[step:] - prod[base + step :, n:]
+    return jnp.concatenate(done, 0)
+
+
+def inverse_kernel(near_ref, far_ref, core_ref, inverse_ref):
+    first = core_ref[0] == 0
+    near, far = near_ref[...], far_ref[...]
+    gram = jnp.concatenate([jnp.where(first, near, far), jnp.where(first, far, near)], 0)
+    gram = (gram + gram.T) * 0.5
+    inverse_ref[...] = inverse_factor(gram)
+
+
+def inverse_of_factor(near, far, core):
+    n = near.shape[1]
+    return pl.pallas_call(
+        inverse_kernel,
+        out_shape=jax.ShapeDtypeStruct((n, n), jnp.float32),
+        in_specs=[
+            pl.BlockSpec(memory_space=pltpu.VMEM),
+            pl.BlockSpec(memory_space=pltpu.VMEM),
+            pl.BlockSpec(memory_space=pltpu.SMEM),
+        ],
+        out_specs=pl.BlockSpec(memory_space=pltpu.VMEM),
+        compiler_params=pltpu.CompilerParams(vmem_limit_bytes=32 * 2**20),
+        cost_estimate=pl.CostEstimate(
+            flops=9_000_000_000, bytes_accessed=1_000_000, transcendentals=128
+        ),
+    )(near, far, core.reshape(1))
 
 
 def per_device(genotypes, probes, missing_codes):
@@ -131,22 +219,15 @@
         half, probe_count
     )
     gram_other = swapped(gram_half)
-    gram = jnp.where(
-        core == 0,
-        jnp.concatenate([gram_half, gram_other]),
-        jnp.concatenate([gram_other, gram_half]),
-    )
-    lower = jnp.linalg.cholesky(gram)
-    inverse = jax.scipy.linalg.solve_triangular(
-        lower, jnp.eye(probe_count, dtype=jnp.float32), lower=True
-    )
-    basis = jnp.dot(image.astype(jnp.float32), inverse.T, precision=lax.Precision.HIGHEST)
+    inverse = inverse_of_factor(gram_half, gram_other, core)
+    cross_half, inverse = lax.optimization_barrier((cross_half, inverse))
     cross_other = swapped(cross_half)
     cross = jnp.where(
         core == 0,
         jnp.concatenate([cross_half, cross_other]),
         jnp.concatenate([cross_other, cross_half]),
     )
+    basis = jnp.dot(image.astype(jnp.float32), inverse.T, precision=lax.Precision.HIGHEST)
     scores = jnp.dot(cross, inverse.T, precision=lax.Precision.HIGHEST)
     return (
         (basis * math.sqrt(total_rows)).astype(jnp.bfloat16),

time: 183 us -> 170 us (0.929)
  other arithmetic: 28.3 us -> 5.35 us
  Pallas kernels: 0 us -> 9.06 us
    another operation x5 -> x0, other arithmetic: 22.9 us -> none  [the longest x3 12.4 us: per_device(): lower = jnp.linalg.cholesky(gram)]
    pallas_call x0 -> x1, Pallas kernels: none -> 9.06 us  [inverse_of_factor(): pl.pallas_call(inverse_kernel, out_shape=jax.ShapeDtypeStruct((n, n), jnp...]
  transfers between devices with their start and end apart: 6 -> 6, of which waited for: 3 -> 5; matrix products, arithmetic and copies ran while one was open for 14% -> 1% of each run, Pallas kernels for 0% -> 5%
where the time goes in v2:
time: 170 us; the launch traced here: 169 us
  blocking collectives  106 us (62%)
  starting transfers between devices  32.5 us (19%)
  Pallas kernels  9.06 us (5%)
  matrix products  8.53 us (5%)
  other arithmetic  5.35 us (3%)
  waiting for transfers between devices  5.35 us (3%)
    all_to_all x9, blocking collectives, exchanged(): return lax.all_to_all(blocks, axis, 0, 0, tiled=True)  106 us
    ppermute x5, starting transfers between devices, swapped(): return lax.ppermute(array, 'c', SWAP)  28.9 us
    pallas_call x1, Pallas kernels, inverse_of_factor(): pl.pallas_call(inverse_kernel, out_shape=jax.ShapeDtypeStruct((n, n), jnp...  9.06 us
    ppermute x5, waiting for transfers between devices, swapped(): return lax.ppermute(array, 'c', SWAP)  5 us
    reduce_sum x1, other arithmetic, per_device(): square = jnp.sum(dosage * dosage, 0).reshape(blocks, BLOCK_SNPS)  3.69 us
    all_to_all x1, starting transfers between devices, exchanged(): return lax.all_to_all(blocks, axis, 0, 0, tiled=True)  3.65 us
  transfers between devices with their start and end apart: 6, of which 5 were waited for; matrix products, arithmetic and copies ran while one was open for 1% of the time, Pallas kernels for 5%

profile of v2, /device:TPU:1, one launch (start us, length us, event | category | flops | bytes accessed | tf_op | source)
XLA Modules:
  0.0 169.1 jit_solution(2728020636177306465)
XLA Ops:
  0.6 0.0 copy-start
  0.6 0.0 copy-start.3
  0.7 0.0 copy-start.1
  0.7 3.7 %fusion = (f32[2048]{0:T(1024)S(1)}, f32[2048]{0:T(1024)S(1)}) fusion(bf16[960,2048]{1,0:T(8,128)(2,1)} %param.3, s32[960]{0:T(1024)} %param.5, s32[2048]{0:T(1024)S(1)} %add_select_fusion), kind=kLoop, calls=%fused_computation.4 | loop fusion | flops 11792384 | bytes 3960576 | tf_op jit(solution)/shard_map/reduce_sum | solution.py:137
  4.4 0.0 copy-done
  4.4 0.0 copy-done.3
  4.4 0.0 copy-done.1
  4.4 1.6 fusion.35
  6.0 0.2 fusion.17
  6.2 0.1 convert_reduce_fusion.1
  6.3 0.1 dynamic-slice_dynamic-update-slice_fusion
  6.4 0.1 fusion.38
  6.5 0.1 constant_dynamic-update-slice_fusion.4
  6.6 8.8 %collective-permute-start = (f32[1056,128]{1,0:T(8,128)S(1)}, f32[1056,128]{1,0:T(8,128)S(1)}, u32[]{:S(2)}, u32[]{:S(2)}) collective-permute-start(f32[1056,128]{1,0:T(8,128)S(1)} %constant_dynamic-update-slice_fusion.4), channel_id=1, source_target_pairs={{0,32},{32,0},{1,33},{33,1},{2,34},{34,2},{3,35},{35,3},{4,36},{36... | collective-permute-start | bytes 1622024 | tf_op jit(solution)/shard_map/ppermute | solution.py:31
  15.4 0.1 constant_dynamic-update-slice_fusion
  15.4 1.5 collective-permute-done
  16.9 0.1 add.57
  17.0 11.8 %all_to_all.50 = f32[4,264,128]{2,1,0:T(8,128)S(1)} all-to-all(f32[4,264,128]{2,1,0:T(8,128)S(1)} %bitcast.64), channel_id=1, replica_groups=mesh['z'=8,'c'=2,'y'=8,'x'=4] {'x'}, dimensions={0} | all-to-all | bytes 1081344 | tf_op jit(solution)/shard_map/all_to_all | solution.py:17
  28.8 10.7 %all_to_all.51 = f32[8,33,128]{2,1,0:T(8,128)S(1)} all-to-all(f32[8,33,128]{2,1,0:T(8,128)S(1)} %reshape.156), channel_id=1, replica_groups=mesh['z'=8,'c'=2,'y'=8,'x'=4] {'y'}, dimensions={0} | all-to-all | bytes 270336 | tf_op jit(solution)/shard_map/all_to_all | solution.py:17
  39.5 18.2 %all_to_all.52 = f32[8,33,128]{2,1,0:T(8,128)S(1)} all-to-all(f32[8,33,128]{2,1,0:T(8,128)S(1)} %broadcast_in_dim.27), channel_id=1, replica_groups=mesh['z'=8,'c'=2,'y'=8,'x'=4] {'z'}, dimensions={0} | all-to-all | bytes 270336 | tf_op jit(solution)/shard_map/all_to_all | solution.py:17
  57.8 10.7 %all_to_all.53 = f32[8,33,128]{2,1,0:T(8,128)S(1)} all-to-all(f32[8,33,128]{2,1,0:T(8,128)S(1)} %broadcast_in_dim.28), channel_id=1, replica_groups=mesh['z'=8,'c'=2,'y'=8,'x'=4] {'y'}, dimensions={0} | all-to-all | bytes 270336 | tf_op jit(solution)/shard_map/all_to_all | solution.py:17
  68.5 9.4 %all_to_all.54 = f32[4,264,128]{2,1,0:T(8,128)S(1)} all-to-all(f32[4,264,128]{2,1,0:T(8,128)S(1)} %broadcast_in_dim.30), channel_id=1, replica_groups=mesh['z'=8,'c'=2,'y'=8,'x'=4] {'x'}, dimensions={0} | all-to-all | bytes 1081344 | tf_op jit(solution)/shard_map/all_to_all | solution.py:17
  77.9 8.5 %collective-permute-start.1 = (f32[1056,128]{1,0:T(8,128)S(1)}, f32[1056,128]{1,0:T(8,128)S(1)}, u32[]{:S(2)}, u32[]{:S(2)}) collective-permute-start(f32[1056,128]{1,0:T(8,128)S(1)} %bitcast.65), channel_id=1, source_target_pairs={{0,32},{32,0},{1,33},{33,1},{2,34},{34,2},{3,35},{35,3},{4,36},{36... | collective-permute-start | bytes 1622024 | tf_op jit(solution)/shard_map/ppermute | solution.py:31
  86.3 0.0 copy-start.2
  86.4 1.5 collective-permute-done.1
  87.9 0.1 broadcast_select_fusion.1
  88.1 1.1 fusion.7
  89.2 0.0 copy-done.2
  89.2 1.7 %fusion.4 = bf16[960,128]{1,0:T(8,128)(2,1)S(1)} fusion(bf16[2048,128]{1,0:T(8,128)(2,1)S(1)} %fusion.7, bf16[960,2048]{1,0:T(8,128)(2,1)S(1)} %copy-done.2, f32[2048]{0:T(1024)S(1)} %fusion.25, f32[2048]{0:T(1024)S(1)} %fusion.21, s32[2048]{0:T(1024)S(1)} %add_select_fusion, s32[960]{0:T(1024)S(1)} %copy-done.3), kind=kOutput, calls=%fused_computation.11 | convolution fusion | flops 515358720 | bytes 4730624 | tf_op jit(solution)/shard_map/dot_general | solution.py:182
  91.0 1.9 %fusion.14 = f32[2048,128]{1,0:T(8,128)S(1)} fusion(bf16[960,128]{1,0:T(8,128)(2,1)S(1)} %fusion.4, bf16[960,2048]{1,0:T(8,128)(2,1)S(1)} %copy-done.2, f32[2048]{0:T(1024)S(1)} %fusion.25, f32[2048]{0:T(1024)S(1)} %fusion.21, s32[2048]{0:T(1024)S(1)} %add_select_fusion, s32[960]{0:T(1024)S(1)} %copy-done.3), kind=kOutput, calls=%fused_computation.31 | convolution fusion | flops 515112960 | bytes 5254912 | tf_op jit(solution)/shard_map/rs,rb->sb/dot_general | solution.py:185
  92.9 0.3 fusion.39
  93.1 0.1 constant_dynamic-slice_fusion.3
  93.3 2.3 %collective-permute-start.2 = (f32[1088,128]{1,0:T(8,128)S(1)}, f32[1088,128]{1,0:T(8,128)S(1)}, u32[]{:S(2)}, u32[]{:S(2)}) collective-permute-start(f32[1088,128]{1,0:T(8,128)S(1)} %pad_maximum_fusion.1), channel_id=1, source_target_pairs={{0,32},{32,0},{1,33},{33,1},{2,34},{34,2},{3,35},{35,3},{4,36},{36... | collective-permute-start | bytes 1671176 | tf_op jit(solution)/shard_map/ppermute | solution.py:31
  95.6 1.6 collective-permute-done.2
  97.2 0.1 maximum_add_fusion
  97.3 13.0 %all_to_all.55 = f32[4,320,128]{2,1,0:T(8,128)S(1)} all-to-all(f32[4,320,128]{2,1,0:T(8,128)S(1)} %pad_maximum_fusion), channel_id=1, replica_groups=mesh['z'=8,'c'=2,'y'=8,'x'=4] {'x'}, dimensions={0} | all-to-all | bytes 1310720 | tf_op jit(solution)/shard_map/all_to_all | solution.py:17
  110.5 10.5 %all_to_all.56 = f32[8,40,128]{2,1,0:T(8,128)S(1)} all-to-all(f32[8,40,128]{2,1,0:T(8,128)S(1)} %pad_maximum_fusion.2), channel_id=1, replica_groups=mesh['z'=8,'c'=2,'y'=8,'x'=4] {'y'}, dimensions={0} | all-to-all | bytes 327680 | tf_op jit(solution)/shard_map/all_to_all | solution.py:17
  121.0 10.8 %all_to_all.57 = f32[8,40,128]{2,1,0:T(8,128)S(1)} all-to-all(f32[8,40,128]{2,1,0:T(8,128)S(1)} %broadcast_in_dim.32), channel_id=1, replica_groups=mesh['z'=8,'c'=2,'y'=8,'x'=4] {'z'}, dimensions={0} | all-to-all | bytes 327680 | tf_op jit(solution)/shard_map/all_to_all | solution.py:17
  131.8 10.8 %all_to_all.58 = f32[8,40,128]{2,1,0:T(8,128)S(1)} all-to-all(f32[8,40,128]{2,1,0:T(8,128)S(1)} %broadcast_in_dim.33), channel_id=1, replica_groups=mesh['z'=8,'c'=2,'y'=8,'x'=4] {'y'}, dimensions={0} | all-to-all | bytes 327680 | tf_op jit(solution)/shard_map/all_to_all | solution.py:17
  142.5 6.7 %collective-permute-start.3 = (f32[64,128]{1,0:T(8,128)S(1)}, f32[64,128]{1,0:T(8,128)S(1)}, u32[]{:S(2)}, u32[]{:S(2)}) collective-permute-start(f32[64,128]{1,0:T(8,128)S(1)} %slice_bitcast_fusion.near_ref), channel_id=1, source_target_pairs={{0,32},{32,0},{1,33},{33,1},{2,34},{34,2},{3,35},{35,3},{4,36},{36... | collective-permute-start | bytes 98312 | tf_op jit(solution)/shard_map/ppermute | solution.py:31
  149.2 0.8 broadcast_in_dim.35
  150.1 3.7 %all-to-all-start.9 = ((f32[4,256,128]{2,1,0:T(8,128)}), f32[4,256,128]{2,1,0:T(8,128)S(1)}, u32[]{:S(2)}, u32[]{:S(2)}) async-start(f32[4,256,128]{2,1,0:T(8,128)} %broadcast_in_dim.35), calls=%async_computation.9 | async-start | bytes 1048576 | tf_op jit(solution)/shard_map/all_to_all | solution.py:17
  153.7 0.0 collective-permute-done.3.far_ref
  153.7 9.1 %shard_map.50 = f32[128,128]{1,0:T(8,128)S(1)} custom-call(f32[64,128]{1,0:T(8,128)S(1)} %slice_bitcast_fusion.near_ref, f32[64,128]{1,0:T(8,128)S(1)} %collective-permute-done.3.far_ref, s32[1]{0:T(128)} %bitcast.21.core_ref), custom_call_target="tpu_custom_call" | custom-call | flops 8999999488 | bytes 1000000 | tf_op jit(solution)/shard_map/pallas_call | solution.py:104
  162.8 0.3 all-to-all-done.9
  163.1 2.7 %collective-permute-start.4 = (f32[1024,128]{1,0:T(8,128)S(1)}, f32[1024,128]{1,0:T(8,128)S(1)}, u32[]{:S(2)}, u32[]{:S(2)}) collective-permute-start(f32[1024,128]{1,0:T(8,128)S(1)} %bitcast.68), channel_id=1, source_target_pairs={{0,32},{32,0},{1,33},{33,1},{2,34},{34,2},{3,35},{35,3},{4,36},{36... | collective-permute-start | bytes 1572872 | tf_op jit(solution)/shard_map/ppermute | solution.py:31
  165.8 1.1 fusion.3
  166.9 0.4 collective-permute-done.4
  167.4 1.8 %fusion.2 = bf16[2048,128]{1,0:T(8,128)(2,1)} fusion(f32[128,128]{1,0:T(8,128)S(1)} %shard_map.50, f32[1024,128]{1,0:T(8,128)S(1)} %collective-permute-done.4, f32[1024,128]{1,0:T(8,128)S(1)} %bitcast.69, pred[]{:T(512)S(6)} %eq.2), kind=kOutput, calls=%fused_computation.7 | convolution fusion | flops 403963904 | bytes 1638401 | tf_op jit(solution)/shard_map/dot_general | solution.py:231
  (36 shorter events, 0.6 us)
Async XLA Ops:
  0.6 3.8 %copy-start = (bf16[960,128]{1,0:T(8,128)(2,1)S(1)}, bf16[960,128]{1,0:T(8,128)(2,1)}, u32[]{:S(2)}) copy-start(bf16[960,128]{1,0:T(8,128)(2,1)} %param.4) | copy-start | bytes 737284
  0.6 3.8 %copy-start.3 = (s32[960]{0:T(1024)S(1)}, s32[960]{0:T(1024)}, u32[]{:S(2)}) copy-start(s32[960]{0:T(1024)} %param.5) | copy-start | bytes 11524
  0.7 3.7 %copy-start.1 = (bf16[960,2048]{1,0:T(8,128)(2,1)S(1)}, bf16[960,2048]{1,0:T(8,128)(2,1)}, u32[]{:S(2)}) copy-start(bf16[960,2048]{1,0:T(8,128)(2,1)} %param.3) | copy-start | bytes 11796484
  6.6 10.3 %collective-permute-start = (f32[1056,128]{1,0:T(8,128)S(1)}, f32[1056,128]{1,0:T(8,128)S(1)}, u32[]{:S(2)}, u32[]{:S(2)}) collective-permute-start(f32[1056,128]{1,0:T(8,128)S(1)} %constant_dynamic-update-slice_fusion.4), channel_id=1, source_target_pairs={{0,32},{32,0},{1,33},{33,1},{2,34},{34,2},{3,35},{35,3},{4,36},{36... | collective-permute-start | bytes 1622024 | tf_op jit(solution)/shard_map/ppermute | solution.py:31
  77.9 10.0 %collective-permute-start.1 = (f32[1056,128]{1,0:T(8,128)S(1)}, f32[1056,128]{1,0:T(8,128)S(1)}, u32[]{:S(2)}, u32[]{:S(2)}) collective-permute-start(f32[1056,128]{1,0:T(8,128)S(1)} %bitcast.65), channel_id=1, source_target_pairs={{0,32},{32,0},{1,33},{33,1},{2,34},{34,2},{3,35},{35,3},{4,36},{36... | collective-permute-start | bytes 1622024 | tf_op jit(solution)/shard_map/ppermute | solution.py:31
  86.3 2.9 %copy-start.2 = (bf16[960,2048]{1,0:T(8,128)(2,1)S(1)}, bf16[960,2048]{1,0:T(8,128)(2,1)}, u32[]{:S(2)}) copy-start(bf16[960,2048]{1,0:T(8,128)(2,1)} %param.3) | copy-start | bytes 11796484
  93.3 3.9 %collective-permute-start.2 = (f32[1088,128]{1,0:T(8,128)S(1)}, f32[1088,128]{1,0:T(8,128)S(1)}, u32[]{:S(2)}, u32[]{:S(2)}) collective-permute-start(f32[1088,128]{1,0:T(8,128)S(1)} %pad_maximum_fusion.1), channel_id=1, source_target_pairs={{0,32},{32,0},{1,33},{33,1},{2,34},{34,2},{3,35},{35,3},{4,36},{36... | collective-permute-start | bytes 1671176 | tf_op jit(solution)/shard_map/ppermute | solution.py:31
  142.5 11.2 %collective-permute-start.3 = (f32[64,128]{1,0:T(8,128)S(1)}, f32[64,128]{1,0:T(8,128)S(1)}, u32[]{:S(2)}, u32[]{:S(2)}) collective-permute-start(f32[64,128]{1,0:T(8,128)S(1)} %slice_bitcast_fusion.near_ref), channel_id=1, source_target_pairs={{0,32},{32,0},{1,33},{33,1},{2,34},{34,2},{3,35},{35,3},{4,36},{36... | collective-permute-start | bytes 98312 | tf_op jit(solution)/shard_map/ppermute | solution.py:31
  150.1 13.1 %all-to-all-start.9 = ((f32[4,256,128]{2,1,0:T(8,128)}), f32[4,256,128]{2,1,0:T(8,128)S(1)}, u32[]{:S(2)}, u32[]{:S(2)}) async-start(f32[4,256,128]{2,1,0:T(8,128)} %broadcast_in_dim.35), calls=%async_computation.9 | async-start | bytes 1048576 | tf_op jit(solution)/shard_map/all_to_all | solution.py:17
  163.1 4.2 %collective-permute-start.4 = (f32[1024,128]{1,0:T(8,128)S(1)}, f32[1024,128]{1,0:T(8,128)S(1)}, u32[]{:S(2)}, u32[]{:S(2)}) collective-permute-start(f32[1024,128]{1,0:T(8,128)S(1)} %bitcast.68), channel_id=1, source_target_pairs={{0,32},{32,0},{1,33},{33,1},{2,34},{34,2},{3,35},{35,3},{4,36},{36... | collective-permute-start | bytes 1572872 | tf_op jit(solution)/shard_map/ppermute | solution.py:31

commit v3 on v2

--- a/solution.py
+++ b/solution.py
@@ -117,83 +117,228 @@
     )(near, far, core.reshape(1))
 
 
+VMEM = pltpu.CompilerParams(vmem_limit_bytes=48 * 2**20)
+COLUMNS = 512
+EXTRA = 32
+
+
+def rows_sum(a, b):
+    return lax.dot_general(a, b, (((0,), (0,)), ((), ())), preferred_element_type=jnp.float32)
+
+
+def moments_kernel(half_ref, genotypes_ref, probes_ref, codes_ref, out_ref, codes_scratch):
+    step = pl.program_id(0)
+    per_step = COLUMNS // BLOCK_SNPS
+    half_blocks = pl.num_programs(0) * per_step
+    half = half_blocks * BLOCK_SNPS
+    first_block = half_ref[0] * half_blocks
+    rows = probes_ref.shape[0]
+
+    @pl.when(step == 0)
+    def _():
+        codes_scratch[...] = jnp.broadcast_to(codes_ref[...], codes_scratch.shape)
+        lane = lax.broadcasted_iota(jnp.int32, (rows, BLOCK_SNPS), 1)
+        seen = (codes_scratch[...] != first_block + lane).astype(jnp.float32).astype(jnp.bfloat16)
+        sums = rows_sum(seen, probes_ref[...])
+        counts = rows_sum(seen, jnp.ones((rows, BLOCK_SNPS), jnp.bfloat16))
+        out_ref[pl.ds(half + 2 * half_blocks, half_blocks)] = sums[:half_blocks]
+        out_ref[pl.ds(half + 3 * half_blocks, half_blocks)] = counts[:half_blocks]
+
+    for i in range(per_step):
+        block = step * per_step + i
+        seen = codes_scratch[...] != first_block + block
+        dosage = jnp.where(
+            seen, genotypes_ref[:, i * BLOCK_SNPS : (i + 1) * BLOCK_SNPS].astype(jnp.float32), 0.0
+        )
+        out_ref[pl.ds(pl.multiple_of(block * BLOCK_SNPS, BLOCK_SNPS), BLOCK_SNPS)] = rows_sum(
+            dosage.astype(jnp.bfloat16), probes_ref[...]
+        )
+        out_ref[pl.ds(half + block, 1)] = jnp.sum(dosage, 0, keepdims=True)
+        out_ref[pl.ds(half + half_blocks + block, 1)] = jnp.sum(dosage * dosage, 0, keepdims=True)
+
+
+def moments(which, genotypes, probes, codes):
+    rows, snps = genotypes.shape
+    half = snps // 2
+    steps = half // COLUMNS
+    return pl.pallas_call(
+        moments_kernel,
+        grid_spec=pltpu.PrefetchScalarGridSpec(
+            num_scalar_prefetch=1,
+            grid=(steps,),
+            in_specs=[
+                pl.BlockSpec((rows, COLUMNS), lambda i, h: (0, h[0] * steps + i)),
+                pl.BlockSpec(probes.shape, lambda i, h: (0, 0)),
+                pl.BlockSpec(codes.shape, lambda i, h: (0, 0)),
+            ],
+            out_specs=pl.BlockSpec((half + EXTRA, BLOCK_SNPS), lambda i, h: (0, 0)),
+            scratch_shapes=[pltpu.VMEM((rows, BLOCK_SNPS), jnp.int32)],
+        ),
+        out_shape=jax.ShapeDtypeStruct((half + EXTRA, BLOCK_SNPS), jnp.float32),
+        compiler_params=VMEM,
+        cost_estimate=pl.CostEstimate(
+            flops=1_500_000_000, bytes_accessed=3_000_000, transcendentals=0
+        ),
+    )(which.reshape(1), genotypes, probes, codes)
+
+
+def image_kernel(
+    total_rows, core_ref, mine_ref, other_ref, genotypes_ref, codes_ref,
+    standard_ref, image_ref, gram_ref, codes_scratch, projection, image_sum,
+):
+    step = pl.program_id(0)
+    steps = pl.num_programs(0)
+    per_step = COLUMNS // BLOCK_SNPS
+    half_blocks = steps * per_step // 2
+    half = half_blocks * BLOCK_SNPS
+    snps = 2 * half
+
+    @pl.when(step == 0)
+    def _():
+        codes_scratch[...] = jnp.broadcast_to(codes_ref[...], codes_scratch.shape)
+
+    own = (core_ref[0] == 0) == (step < steps // 2)
+    for i in range(per_step):
+        block = step * per_step + i
+        local = lax.rem(step, steps // 2) * per_step + i
+
+        def row(start):
+            at = pl.ds(start, 1)
+            return jnp.where(own, mine_ref[at], other_ref[at])
+
+        counted = jnp.maximum(row(half + 3 * half_blocks + local), 1.0)
+        mean = row(half + local) / counted
+        inv_sd = 1.0 / jnp.sqrt(
+            row(half + half_blocks + local) / counted - mean * mean + 1e-05
+        )
+        square = (BLOCK_SNPS, BLOCK_SNPS)
+        mean_down = jnp.broadcast_to(mean, square).T
+        inv_sd_down = jnp.broadcast_to(inv_sd, square).T
+        at = pl.ds(pl.multiple_of(local * BLOCK_SNPS, BLOCK_SNPS), BLOCK_SNPS)
+        raw = jnp.where(own, mine_ref[at], other_ref[at])
+        centred = raw - mean_down * row(half + 2 * half_blocks + local)
+        here = slice(i * BLOCK_SNPS, (i + 1) * BLOCK_SNPS)
+        projection[here] = (centred * inv_sd_down * (1.0 / math.sqrt(total_rows))).astype(
+            jnp.bfloat16
+        )
+        scaled = (genotypes_ref[:, here].astype(jnp.float32) - mean) * inv_sd
+        standard_ref[:, here] = jnp.where(codes_scratch[...] != block, scaled, 0.0).astype(
+            jnp.bfloat16
+        )
+    part = jnp.dot(standard_ref[...], projection[...], preferred_element_type=jnp.float32)
+
+    @pl.when(step == 0)
+    def _():
+        image_sum[...] = part
+
+    @pl.when(step > 0)
+    def _():
+        image_sum[...] += part
+
+    @pl.when(step == steps - 1)
+    def _():
+        image = (image_sum[...] * (1.0 / math.sqrt(snps))).astype(jnp.bfloat16)
+        image_ref[...] = image
+        gram_ref[...] = rows_sum(image, image)
+
+
+def images(total_rows, core, mine, other, genotypes, codes):
+    rows, snps = genotypes.shape
+    probe_count = mine.shape[1]
+    return pl.pallas_call(
+        lambda *refs: image_kernel(total_rows, *refs),
+        grid_spec=pltpu.PrefetchScalarGridSpec(
+            num_scalar_prefetch=1,
+            grid=(snps // COLUMNS,),
+            in_specs=[
+                pl.BlockSpec(mine.shape, lambda i, c: (0, 0)),
+                pl.BlockSpec(other.shape, lambda i, c: (0, 0)),
+                pl.BlockSpec((rows, COLUMNS), lambda i, c: (0, i)),
+                pl.BlockSpec(codes.shape, lambda i, c: (0, 0)),
+            ],
+            out_specs=[
+                pl.BlockSpec((rows, COLUMNS), lambda i, c: (0, i)),
+                pl.BlockSpec((rows, probe_count), lambda i, c: (0, 0)),
+                pl.BlockSpec((probe_count, probe_count), lambda i, c: (0, 0)),
+            ],
+            scratch_shapes=[
+                pltpu.VMEM((rows, BLOCK_SNPS), jnp.int32),
+                pltpu.VMEM((COLUMNS, probe_count), jnp.bfloat16),
+                pltpu.VMEM((rows, probe_count), jnp.float32),
+            ],
+        ),
+        out_shape=(
+            jax.ShapeDtypeStruct((rows, snps), jnp.bfloat16),
+            jax.ShapeDtypeStruct((rows, probe_count), jnp.bfloat16),
+            jax.ShapeDtypeStruct((probe_count, probe_count), jnp.float32),
+        ),
+        compiler_params=VMEM,
+        cost_estimate=pl.CostEstimate(
+            flops=2_500_000_000, bytes_accessed=9_000_000, transcendentals=0
+        ),
+    )(core.reshape(1), mine, other, genotypes, codes)
+
+
+def cross_kernel(which_ref, standard_ref, image_ref, gram_ref, out_ref):
+    step = pl.program_id(0)
+    out_ref[pl.ds(pl.multiple_of(step * COLUMNS, COLUMNS), COLUMNS)] = rows_sum(
+        standard_ref[...], image_ref[...]
+    )
+
+    @pl.when(step == 0)
+    def _():
+        n = gram_ref.shape[0] // 2
+        out_ref[pl.ds(pl.num_programs(0) * COLUMNS, n)] = gram_ref[
+            pl.ds(pl.multiple_of(which_ref[0] * n, n), n)
+        ]
+
+
+def crossed(which, standard, image, gram):
+    rows, snps = standard.shape
+    half = snps // 2
+    steps = half // COLUMNS
+    n = image.shape[1]
+    return pl.pallas_call(
+        cross_kernel,
+        grid_spec=pltpu.PrefetchScalarGridSpec(
+            num_scalar_prefetch=1,
+            grid=(steps,),
+            in_specs=[
+                pl.BlockSpec((rows, COLUMNS), lambda i, h: (0, h[0] * steps + i)),
+                pl.BlockSpec(image.shape, lambda i, h: (0, 0)),
+                pl.BlockSpec(gram.shape, lambda i, h: (0, 0)),
+            ],
+            out_specs=pl.BlockSpec((half + n // 2, n), lambda i, h: (0, 0)),
+        ),
+        out_shape=jax.ShapeDtypeStruct((half + n // 2, n), jnp.float32),
+        compiler_params=VMEM,
+        cost_estimate=pl.CostEstimate(
+            flops=1_200_000_000, bytes_accessed=3_000_000, transcendentals=0
+        ),
+    )(which.reshape(1), standard, image, gram)
+
+
 def per_device(genotypes, probes, missing_codes):
     rows, snps = genotypes.shape
     probe_count = probes.shape[1]
     total_rows = rows * math.prod(lax.axis_size(a) for a in ALL)
     core = lax.axis_index("c")
-    blocks = snps // BLOCK_SNPS
     half = snps // 2
-    block_half = blocks // 2
     wide_x, wide_y = lax.axis_size("x"), lax.axis_size("y")
-
-    snp_block = jnp.arange(snps) // BLOCK_SNPS
-    seen = snp_block[None, :] != missing_codes[:, None]
-    observed = seen.astype(jnp.float32)
-    kept = jnp.where(seen, genotypes, jnp.zeros_like(genotypes))
-    dosage = kept.astype(jnp.float32)
-    raw = jnp.einsum("rs,rb->sb", kept, probes, preferred_element_type=jnp.float32)
-    total = jnp.sum(dosage, 0).reshape(blocks, BLOCK_SNPS)
-    square = jnp.sum(dosage * dosage, 0).reshape(blocks, BLOCK_SNPS)
-    by_block = jnp.arange(blocks)[None, :] != missing_codes[:, None]
-    seen_probes = jnp.einsum(
-        "rk,rb->kb", by_block.astype(jnp.bfloat16), probes, preferred_element_type=jnp.float32
-    )
-    count = jnp.broadcast_to(
-        jnp.sum(by_block.astype(jnp.float32), 0)[:, None], (blocks, BLOCK_SNPS)
-    )
-
-    def part(which):
-        def take(a):
-            n = a.shape[0] // 2
-            return lax.dynamic_slice_in_dim(a, which * n, n)
-
-        return jnp.concatenate([take(a) for a in (raw, total, square, seen_probes, count)])
-
-    mine = part(core) + swapped(part(1 - core))
+    codes = missing_codes.reshape(rows, 1)
+
+    sent = moments(1 - core, genotypes, probes, codes)
+    mine = moments(core, genotypes, probes, codes) + swapped(sent)
     mine = summed_parts(mine, "x")
     mine = summed_parts(mine, "y")
     mine = jnp.sum(copies(mine, "z"), 0)
     mine = copies(mine, "y").reshape(-1, probe_count)
     mine = copies(mine, "x").reshape(-1, probe_count)
-    other = swapped(mine)
-    first = jnp.where(core == 0, mine, other)
-    second = jnp.where(core == 0, other, mine)
-
-    def joined(start, length):
-        return jnp.concatenate([first[start : start + length], second[start : start + length]])
-
-    raw = joined(0, half)
-    total, square, seen_probes, count = (
-        joined(half + i * block_half, block_half) for i in range(4)
-    )
-    counted = jnp.maximum(count, 1.0)
-    mean = total / counted
-    inv_sd = 1.0 / jnp.sqrt(square / counted - mean * mean + 1e-05)
-    centred = (
-        raw.reshape(blocks, BLOCK_SNPS, probe_count) - mean[:, :, None] * seen_probes[:, None, :]
-    )
-    projection = (centred * inv_sd[:, :, None] / math.sqrt(total_rows)).astype(jnp.bfloat16)
-    projection = projection.reshape(snps, probe_count)
-    standard = (
-        (genotypes.astype(jnp.float32) - mean.reshape(1, snps)) * inv_sd.reshape(1, snps) * observed
-    ).astype(jnp.bfloat16)
-    image = (
-        jnp.dot(standard, projection, preferred_element_type=jnp.float32) / math.sqrt(snps)
-    ).astype(jnp.bfloat16)
-    gram = jnp.einsum("rb,rc->bc", image, image, preferred_element_type=jnp.float32)
-    cross = jnp.einsum("rs,rb->sb", standard, image, preferred_element_type=jnp.float32)
-
-    def halves(which):
-        n = probe_count // 2
-        return jnp.concatenate(
-            [
-                lax.dynamic_slice_in_dim(cross, which * half, half),
-                lax.dynamic_slice_in_dim(gram, which * n, n),
-            ]
-        )
-
-    mine = halves(core) + swapped(halves(1 - core))
+    standard, image, gram = images(
+        total_rows, core, mine, swapped(mine), genotypes, codes
+    )
+    sent = crossed(1 - core, standard, image, gram)
+    mine = crossed(core, standard, image, gram) + swapped(sent)
     over_x = jnp.concatenate(
         [
             mine[:half].reshape(wide_x, half // wide_x, probe_count),

time: 170 us -> 172 us (1.012)
  Pallas kernels: 9.06 us -> 21.3 us
  matrix products: 8.53 us -> 2.85 us
  other arithmetic: 5.35 us -> 0.29 us
  local copies, waits for them, and re-layouts: 1.53 us -> 5.02 us
  waiting for transfers between devices: 5.35 us -> 2.88 us
    pallas_call x0 -> x5, Pallas kernels: none -> 12.2 us  [the longest x1 5.8 us: images(): pl.pallas_call(lambda *refs: image_kernel(total_rows, *refs), grid_spec=p...]
    dot_general x5 -> x0, matrix products: 5.67 us -> none  [the longest x1 1.88 us: per_device(): jnp.einsum('rs,rb->sb', standard, image, preferred_element_type=jnp.float32)]
    reduce_sum x2 -> x0, other arithmetic: 3.82 us -> none  [the longest x1 3.69 us: per_device(): square = jnp.sum(dosage * dosage, 0).reshape(blocks, BLOCK_SNPS)]
    unnamed x12 -> x8, local copies, waits for them, and re-layouts: 0.11 us -> 3.06 us
    ppermute x5, waiting for transfers between devices: 5 us -> 2.35 us  [swapped(): return lax.ppermute(array, 'c', SWAP)]
  transfers between devices with their start and end apart: 6 -> 6, of which waited for: 5 -> 4; matrix products, arithmetic and copies ran while one was open for 1% -> 1% of each run, Pallas kernels for 5% -> 7%
where the time goes in v3:
time: 172 us; the launch traced here: 171 us
  blocking collectives  106 us (62%)
  starting transfers between devices  32 us (19%)
  Pallas kernels  21.3 us (12%)
  local copies, waits for them, and re-layouts  5.02 us (3%)
  waiting for transfers between devices  2.88 us (2%)
  matrix products  2.85 us (2%)
    all_to_all x9, blocking collectives, exchanged(): return lax.all_to_all(blocks, axis, 0, 0, tiled=True)  106 us
    ppermute x5, starting transfers between devices, swapped(): return lax.ppermute(array, 'c', SWAP)  28.6 us
    pallas_call x1, Pallas kernels, inverse_of_factor(): pl.pallas_call(inverse_kernel, out_shape=jax.ShapeDtypeStruct((n, n), jnp...  9.05 us
    pallas_call x1, Pallas kernels, images(): pl.pallas_call(lambda *refs: image_kernel(total_rows, *refs), grid_spec=p...  5.8 us
    pallas_call x2, Pallas kernels, moments(): pl.pallas_call(moments_kernel, grid_spec=pltpu.PrefetchScalarGridSpec(num...  4.03 us
    all_to_all x1, starting transfers between devices, exchanged(): return lax.all_to_all(blocks, axis, 0, 0, tiled=True)  3.47 us
  transfers between devices with their start and end apart: 6, of which 4 were waited for; matrix products, arithmetic and copies ran while one was open for 1% of the time, Pallas kernels for 7%

profile of v3, /device:TPU:1, one launch (start us, length us, event | category | flops | bytes accessed | tf_op | source)
XLA Modules:
  0.0 171.4 jit_solution(14723288809618646690)
XLA Ops:
  0.6 0.0 copy-start.3
  0.6 0.9 copy.11.codes_ref.refs_4_
  1.6 0.0 copy-start
  1.6 2.1 %copy-done = bf16[960,2048]{1,0:T(8,128)(2,1)S(1)} copy-done((bf16[960,2048]{1,0:T(8,128)(2,1)S(1)}, bf16[960,2048]{1,0:T(8,128)(2,1)}, u32[]{:S(2)}) %copy-start) | copy-done | bytes 3932184
  3.7 0.0 copy-start.2
  3.7 0.9 copy-done.2
  4.7 0.0 copy-start.1
  4.7 2.0 %shard_map.51 = f32[1056,128]{1,0:T(8,128)S(1)} custom-call(s32[1]{0:T(128)} %bitcast.2.half_ref.which_ref, bf16[960,2048]{1,0:T(8,128)(2,1)S(1)} %copy-done, bf16[960,128]{1,0:T(8,128)(2,1)S(1)} %copy-done.2, s32[960,1]{1,0:T(8,128)S(1)} %copy.11.codes_ref.refs_4_), custom_call_target="tpu_custom_call" | custom-call | flops 1500000000 | bytes 3000000 | tf_op jit(solution)/shard_map/pallas_call | solution.py:164
  6.7 8.8 %collective-permute-start = (f32[1056,128]{1,0:T(8,128)S(1)}, f32[1056,128]{1,0:T(8,128)S(1)}, u32[]{:S(2)}, u32[]{:S(2)}) collective-permute-start(f32[1056,128]{1,0:T(8,128)S(1)} %shard_map.51), channel_id=1, source_target_pairs={{0,32},{32,0},{1,33},{33,1},{2,34},{34,2},{3,35},{35,3},{4,36},{36... | collective-permute-start | bytes 1622024 | tf_op jit(solution)/shard_map/ppermute | solution.py:31
  15.5 0.0 copy-done.3
  15.5 0.0 copy-done.1
  15.5 2.0 %shard_map.50 = f32[1056,128]{1,0:T(8,128)S(1)} custom-call(s32[1]{0:T(128)} %bitcast.half_ref.refs_0_.which_ref.core_ref, bf16[960,2048]{1,0:T(8,128)(2,1)S(1)} %copy-done.1, bf16[960,128]{1,0:T(8,128)(2,1)S(1)} %copy-done.3, s32[960,1]{1,0:T(8,128)S(1)} %copy.11.codes_ref.refs_4_), custom_call_target="tpu_custom_call" | custom-call | flops 1500000000 | bytes 3000000 | tf_op jit(solution)/shard_map/pallas_call | solution.py:164
  17.5 0.0 collective-permute-done
  17.5 0.1 add.6
  17.6 12.2 %all_to_all.50 = f32[4,264,128]{2,1,0:T(8,128)S(1)} all-to-all(f32[4,264,128]{2,1,0:T(8,128)S(1)} %bitcast.18), channel_id=1, replica_groups=mesh['z'=8,'c'=2,'y'=8,'x'=4] {'x'}, dimensions={0} | all-to-all | bytes 1081344 | tf_op jit(solution)/shard_map/all_to_all | solution.py:17
  29.8 10.4 %all_to_all.51 = f32[8,33,128]{2,1,0:T(8,128)S(1)} all-to-all(f32[8,33,128]{2,1,0:T(8,128)S(1)} %reshape.52), channel_id=1, replica_groups=mesh['z'=8,'c'=2,'y'=8,'x'=4] {'y'}, dimensions={0} | all-to-all | bytes 270336 | tf_op jit(solution)/shard_map/all_to_all | solution.py:17
  40.3 18.4 %all_to_all.52 = f32[8,33,128]{2,1,0:T(8,128)S(1)} all-to-all(f32[8,33,128]{2,1,0:T(8,128)S(1)} %broadcast_in_dim.18), channel_id=1, replica_groups=mesh['z'=8,'c'=2,'y'=8,'x'=4] {'z'}, dimensions={0} | all-to-all | bytes 270336 | tf_op jit(solution)/shard_map/all_to_all | solution.py:17
  58.7 10.7 %all_to_all.53 = f32[8,33,128]{2,1,0:T(8,128)S(1)} all-to-all(f32[8,33,128]{2,1,0:T(8,128)S(1)} %broadcast_in_dim.19), channel_id=1, replica_groups=mesh['z'=8,'c'=2,'y'=8,'x'=4] {'y'}, dimensions={0} | all-to-all | bytes 270336 | tf_op jit(solution)/shard_map/all_to_all | solution.py:17
  69.4 9.4 %all_to_all.54 = f32[4,264,128]{2,1,0:T(8,128)S(1)} all-to-all(f32[4,264,128]{2,1,0:T(8,128)S(1)} %broadcast_in_dim.21), channel_id=1, replica_groups=mesh['z'=8,'c'=2,'y'=8,'x'=4] {'x'}, dimensions={0} | all-to-all | bytes 1081344 | tf_op jit(solution)/shard_map/all_to_all | solution.py:17
  78.8 8.1 %collective-permute-start.1 = (f32[1056,128]{1,0:T(8,128)S(1)}, f32[1056,128]{1,0:T(8,128)S(1)}, u32[]{:S(2)}, u32[]{:S(2)}) collective-permute-start(f32[1056,128]{1,0:T(8,128)S(1)} %bitcast.16), channel_id=1, source_target_pairs={{0,32},{32,0},{1,33},{33,1},{2,34},{34,2},{3,35},{35,3},{4,36},{36... | collective-permute-start | bytes 1622024 | tf_op jit(solution)/shard_map/ppermute | solution.py:31
  87.0 1.5 collective-permute-done.1.refs_2_
  88.5 5.8 %shard_map.52 = (bf16[960,2048]{1,0:T(8,128)(2,1)S(1)}, bf16[960,128]{1,0:T(8,128)(2,1)S(1)}, f32[128,128]{1,0:T(8,128)S(1)}) custom-call(s32[1]{0:T(128)} %bitcast.half_ref.refs_0_.which_ref.core_ref, f32[1056,128]{1,0:T(8,128)S(1)} %bitcast.17, f32[1056,128]{1,0:T(8,128)S(1)} %collective-permute-done.1.refs_2_, bf16[960,2048]{1,0:T(8,128)(2,1)} %refs_3_.1, ...), custom_call_target="tpu_custom_call" | custom-call | flops 2500000000 | bytes 9000000 | tf_op jit(solution)/shard_map/pallas_call | solution.py:248
  94.3 1.2 shard_map.54
  95.5 2.3 %collective-permute-start.2 = (f32[1088,128]{1,0:T(8,128)S(1)}, f32[1088,128]{1,0:T(8,128)S(1)}, u32[]{:S(2)}, u32[]{:S(2)}) collective-permute-start(f32[1088,128]{1,0:T(8,128)S(1)} %shard_map.54), channel_id=1, source_target_pairs={{0,32},{32,0},{1,33},{33,1},{2,34},{34,2},{3,35},{35,3},{4,36},{36... | collective-permute-start | bytes 1671176 | tf_op jit(solution)/shard_map/ppermute | solution.py:31
  97.8 1.2 shard_map.53
  99.0 0.4 collective-permute-done.2
  99.4 0.1 add.7
  99.6 13.0 %all_to_all.55 = f32[4,320,128]{2,1,0:T(8,128)S(1)} all-to-all(f32[4,320,128]{2,1,0:T(8,128)S(1)} %pad_maximum_fusion), channel_id=1, replica_groups=mesh['z'=8,'c'=2,'y'=8,'x'=4] {'x'}, dimensions={0} | all-to-all | bytes 1310720 | tf_op jit(solution)/shard_map/all_to_all | solution.py:17
  112.7 10.5 %all_to_all.56 = f32[8,40,128]{2,1,0:T(8,128)S(1)} all-to-all(f32[8,40,128]{2,1,0:T(8,128)S(1)} %pad_maximum_fusion.1), channel_id=1, replica_groups=mesh['z'=8,'c'=2,'y'=8,'x'=4] {'y'}, dimensions={0} | all-to-all | bytes 327680 | tf_op jit(solution)/shard_map/all_to_all | solution.py:17
  123.2 10.8 %all_to_all.57 = f32[8,40,128]{2,1,0:T(8,128)S(1)} all-to-all(f32[8,40,128]{2,1,0:T(8,128)S(1)} %broadcast_in_dim.23), channel_id=1, replica_groups=mesh['z'=8,'c'=2,'y'=8,'x'=4] {'z'}, dimensions={0} | all-to-all | bytes 327680 | tf_op jit(solution)/shard_map/all_to_all | solution.py:17
  134.0 10.8 %all_to_all.58 = f32[8,40,128]{2,1,0:T(8,128)S(1)} all-to-all(f32[8,40,128]{2,1,0:T(8,128)S(1)} %broadcast_in_dim.24), channel_id=1, replica_groups=mesh['z'=8,'c'=2,'y'=8,'x'=4] {'y'}, dimensions={0} | all-to-all | bytes 327680 | tf_op jit(solution)/shard_map/all_to_all | solution.py:17
  144.8 6.7 %collective-permute-start.3 = (f32[64,128]{1,0:T(8,128)S(1)}, f32[64,128]{1,0:T(8,128)S(1)}, u32[]{:S(2)}, u32[]{:S(2)}) collective-permute-start(f32[64,128]{1,0:T(8,128)S(1)} %slice_bitcast_fusion.near_ref), channel_id=1, source_target_pairs={{0,32},{32,0},{1,33},{33,1},{2,34},{34,2},{3,35},{35,3},{4,36},{36... | collective-permute-start | bytes 98312 | tf_op jit(solution)/shard_map/ppermute | solution.py:31
  151.4 0.8 broadcast_in_dim.52
  152.3 3.5 %all-to-all-start.9 = ((f32[4,256,128]{2,1,0:T(8,128)}), f32[4,256,128]{2,1,0:T(8,128)S(1)}, u32[]{:S(2)}, u32[]{:S(2)}) async-start(f32[4,256,128]{2,1,0:T(8,128)} %broadcast_in_dim.52), calls=%async_computation.9 | async-start | bytes 1048576 | tf_op jit(solution)/shard_map/all_to_all | solution.py:17
  155.8 0.0 collective-permute-done.3.far_ref
  155.8 9.1 %shard_map.55 = f32[128,128]{1,0:T(8,128)S(1)} custom-call(f32[64,128]{1,0:T(8,128)S(1)} %slice_bitcast_fusion.near_ref, f32[64,128]{1,0:T(8,128)S(1)} %collective-permute-done.3.far_ref, s32[1]{0:T(128)} %bitcast.half_ref.refs_0_.which_ref.core_ref), custom_call_target="tpu_custom_call" | custom-call | flops 8999999488 | bytes 1000000 | tf_op jit(solution)/shard_map/pallas_call | solution.py:104
  164.8 0.5 all-to-all-done.9
  165.4 2.7 %collective-permute-start.4 = (f32[1024,128]{1,0:T(8,128)S(1)}, f32[1024,128]{1,0:T(8,128)S(1)}, u32[]{:S(2)}, u32[]{:S(2)}) collective-permute-start(f32[1024,128]{1,0:T(8,128)S(1)} %bitcast.21), channel_id=1, source_target_pairs={{0,32},{32,0},{1,33},{33,1},{2,34},{34,2},{3,35},{35,3},{4,36},{36... | collective-permute-start | bytes 1572872 | tf_op jit(solution)/shard_map/ppermute | solution.py:31
  168.1 1.1 fusion.1
  169.1 0.4 collective-permute-done.4
  169.6 1.8 %fusion = bf16[2048,128]{1,0:T(8,128)(2,1)} fusion(f32[128,128]{1,0:T(8,128)S(1)} %shard_map.55, f32[1024,128]{1,0:T(8,128)S(1)} %collective-permute-done.4, f32[1024,128]{1,0:T(8,128)S(1)} %bitcast.22, pred[]{:T(512)S(6)} %eq.3), kind=kOutput, calls=%fused_computation.1 | convolution fusion | flops 403963904 | bytes 1638401 | tf_op jit(solution)/shard_map/dot_general | solution.py:376
  (22 shorter events, 0.4 us)
Async XLA Ops:
  0.6 14.9 %copy-start.3 = (bf16[960,128]{1,0:T(8,128)(2,1)S(1)}, bf16[960,128]{1,0:T(8,128)(2,1)}, u32[]{:S(2)}) copy-start(bf16[960,128]{1,0:T(8,128)(2,1)} %probes_ref.3) | copy-start | bytes 737284
  1.6 2.1 %copy-start = (bf16[960,2048]{1,0:T(8,128)(2,1)S(1)}, bf16[960,2048]{1,0:T(8,128)(2,1)}, u32[]{:S(2)}) copy-start(bf16[960,2048]{1,0:T(8,128)(2,1)} %refs_3_.1) | copy-start | bytes 11796484
  3.7 0.9 copy-start.2
  4.7 10.9 %copy-start.1 = (bf16[960,2048]{1,0:T(8,128)(2,1)S(1)}, bf16[960,2048]{1,0:T(8,128)(2,1)}, u32[]{:S(2)}) copy-start(bf16[960,2048]{1,0:T(8,128)(2,1)} %refs_3_.1) | copy-start | bytes 11796484
  6.7 10.8 %collective-permute-start = (f32[1056,128]{1,0:T(8,128)S(1)}, f32[1056,128]{1,0:T(8,128)S(1)}, u32[]{:S(2)}, u32[]{:S(2)}) collective-permute-start(f32[1056,128]{1,0:T(8,128)S(1)} %shard_map.51), channel_id=1, source_target_pairs={{0,32},{32,0},{1,33},{33,1},{2,34},{34,2},{3,35},{35,3},{4,36},{36... | collective-permute-start | bytes 1622024 | tf_op jit(solution)/shard_map/ppermute | solution.py:31
  78.8 9.7 %collective-permute-start.1 = (f32[1056,128]{1,0:T(8,128)S(1)}, f32[1056,128]{1,0:T(8,128)S(1)}, u32[]{:S(2)}, u32[]{:S(2)}) collective-permute-start(f32[1056,128]{1,0:T(8,128)S(1)} %bitcast.16), channel_id=1, source_target_pairs={{0,32},{32,0},{1,33},{33,1},{2,34},{34,2},{3,35},{35,3},{4,36},{36... | collective-permute-start | bytes 1622024 | tf_op jit(solution)/shard_map/ppermute | solution.py:31
  95.5 3.9 %collective-permute-start.2 = (f32[1088,128]{1,0:T(8,128)S(1)}, f32[1088,128]{1,0:T(8,128)S(1)}, u32[]{:S(2)}, u32[]{:S(2)}) collective-permute-start(f32[1088,128]{1,0:T(8,128)S(1)} %shard_map.54), channel_id=1, source_target_pairs={{0,32},{32,0},{1,33},{33,1},{2,34},{34,2},{3,35},{35,3},{4,36},{36... | collective-permute-start | bytes 1671176 | tf_op jit(solution)/shard_map/ppermute | solution.py:31
  144.8 11.0 %collective-permute-start.3 = (f32[64,128]{1,0:T(8,128)S(1)}, f32[64,128]{1,0:T(8,128)S(1)}, u32[]{:S(2)}, u32[]{:S(2)}) collective-permute-start(f32[64,128]{1,0:T(8,128)S(1)} %slice_bitcast_fusion.near_ref), channel_id=1, source_target_pairs={{0,32},{32,0},{1,33},{33,1},{2,34},{34,2},{3,35},{35,3},{4,36},{36... | collective-permute-start | bytes 98312 | tf_op jit(solution)/shard_map/ppermute | solution.py:31
  152.3 13.1 %all-to-all-start.9 = ((f32[4,256,128]{2,1,0:T(8,128)}), f32[4,256,128]{2,1,0:T(8,128)S(1)}, u32[]{:S(2)}, u32[]{:S(2)}) async-start(f32[4,256,128]{2,1,0:T(8,128)} %broadcast_in_dim.52), calls=%async_computation.9 | async-start | bytes 1048576 | tf_op jit(solution)/shard_map/all_to_all | solution.py:17
  165.4 4.2 %collective-permute-start.4 = (f32[1024,128]{1,0:T(8,128)S(1)}, f32[1024,128]{1,0:T(8,128)S(1)}, u32[]{:S(2)}, u32[]{:S(2)}) collective-permute-start(f32[1024,128]{1,0:T(8,128)S(1)} %bitcast.21), channel_id=1, source_target_pairs={{0,32},{32,0},{1,33},{33,1},{2,34},{34,2},{3,35},{35,3},{4,36},{36... | collective-permute-start | bytes 1572872 | tf_op jit(solution)/shard_map/ppermute | solution.py:31

commit v4 on v2

--- a/solution.py
+++ b/solution.py
@@ -30,6 +30,57 @@
 def swapped(array):
     return lax.ppermute(array, "c", SWAP)
 
+def panel(upper, under, base, extra):
+    step, n = upper.shape
+    row_of = lax.broadcasted_iota(jnp.int32, (step, n), 0)
+    a = [
+        [
+            jnp.broadcast_to(upper[i : i + 1, base + k : base + k + 1], (step, n))
+            if k >= i
+            else None
+            for k in range(step)
+        ]
+        for i in range(step)
+    ]
+    x = [[None] * step for _ in range(step)]
+    scale = []
+    for t in range(step):
+        r = lax.rsqrt(a[t][t])
+        scale.append(r)
+        u = [None] * step
+        for k in range(t + 1, step):
+            u[k] = a[t][k] * r
+        for i in range(t + 1, step):
+            for k in range(i, step):
+                a[i][k] = a[i][k] - u[i] * u[k]
+        a[t] = u
+    for i in range(step):
+        x[i][i] = scale[i]
+        for k in range(i):
+            s = a[k][i] * x[k][k]
+            for m in range(k + 1, i):
+                s = s + a[m][i] * x[m][k]
+            x[i][k] = -s * scale[i]
+    both = jnp.concatenate([upper, under], 1)
+    out = None
+    for k in range(step):
+        col = jnp.zeros((step, n), jnp.float32)
+        for i in range(k, step):
+            col = jnp.where(row_of == i, x[i][k], col)
+        term = jnp.concatenate([col, col], 1) * both[k : k + 1]
+        out = term if out is None else out + term
+    columns = None
+    if extra is not None:
+        raw = [jnp.broadcast_to(extra[:, base + k : base + k + 1], (step, n)) for k in range(step)]
+        columns = []
+        for t in range(step):
+            s = raw[0] * x[t][0]
+            for k in range(1, t + 1):
+                s = s + raw[k] * x[t][k]
+            columns.append(s)
+    return out, columns
+
+
 def inverse_factor(gram):
     n = gram.shape[0]
     step = 8
@@ -37,57 +88,25 @@
     inv = (
         lax.broadcasted_iota(jnp.int32, (n, n), 0) == lax.broadcasted_iota(jnp.int32, (n, n), 1)
     ).astype(jnp.float32)
-    row_of = lax.broadcasted_iota(jnp.int32, (step, n), 0)
     done = []
-    for base in range(0, n, step):
-        upper = left[:step]
-        under = inv[:step]
-        a = [
-            [
-                jnp.broadcast_to(upper[i : i + 1, base + k : base + k + 1], (step, n))
-                if k >= i
-                else None
-                for k in range(step)
-            ]
-            for i in range(step)
-        ]
-        x = [[None] * step for _ in range(step)]
-        scale = []
+    for base in range(0, n, 2 * step):
+        first, columns = panel(left[:step], inv[:step], base, left[step : 2 * step])
+        both = jnp.concatenate([left[step : 2 * step], inv[step : 2 * step]], 1)
         for t in range(step):
-            r = lax.rsqrt(a[t][t])
-            scale.append(r)
-            u = [None] * step
-            for k in range(t + 1, step):
-                u[k] = a[t][k] * r
-            for i in range(t + 1, step):
-                for k in range(i, step):
-                    a[i][k] = a[i][k] - u[i] * u[k]
-            a[t] = u
-        for i in range(step):
-            x[i][i] = scale[i]
-            for k in range(i):
-                s = a[k][i] * x[k][k]
-                for m in range(k + 1, i):
-                    s = s + a[m][i] * x[m][k]
-                x[i][k] = -s * scale[i]
-        cols = []
-        for k in range(step):
-            col = jnp.zeros((step, n), jnp.float32)
-            for i in range(k, step):
-                col = jnp.where(row_of == i, x[i][k], col)
-            cols.append(col)
-        both = jnp.concatenate([upper, under], 1)
-        out = sum(
-            jnp.concatenate([cols[k], cols[k]], 1) * both[k : k + 1] for k in range(step)
-        )
+            both = both - jnp.concatenate([columns[t], columns[t]], 1) * first[t : t + 1]
+        second, _ = panel(both[:, :n], both[:, n:], base + step, None)
+        out = jnp.concatenate([first, second], 0)
         done.append(out[:, n:])
-        if base + step < n:
-            u = out[:, :n]
+        if base + 2 * step < n:
             prod = lax.dot_general(
-                u, out, (((0,), (0,)), ((), ())), precision=lax.Precision.HIGHEST, preferred_element_type=jnp.float32
+                out[:, :n],
+                out,
+                (((0,), (0,)), ((), ())),
+                precision=lax.Precision.HIGHEST,
+                preferred_element_type=jnp.float32,
             )
-            left = left[step:] - prod[base + step :, :n]
-            inv = inv[step:] - prod[base + step :, n:]
+            left = left[2 * step :] - prod[base + 2 * step :, :n]
+            inv = inv[2 * step :] - prod[base + 2 * step :, n:]
     return jnp.concatenate(done, 0)
 
 
@@ -117,40 +136,82 @@
     )(near, far, core.reshape(1))
 
 
+VMEM = pltpu.CompilerParams(vmem_limit_bytes=60 * 2**20)
+COLUMNS = 512
+EXTRA = 32
+
+
+def rows_sum(a, b):
+    return lax.dot_general(a, b, (((0,), (0,)), ((), ())), preferred_element_type=jnp.float32)
+
+
+def moments_kernel(half_ref, genotypes_ref, probes_ref, codes_ref, out_ref, codes_scratch):
+    step = pl.program_id(0)
+    per_step = COLUMNS // BLOCK_SNPS
+    half_blocks = pl.num_programs(0) * per_step
+    half = half_blocks * BLOCK_SNPS
+    first_block = half_ref[0] * half_blocks
+    rows = probes_ref.shape[0]
+
+    @pl.when(step == 0)
+    def _():
+        codes_scratch[...] = jnp.broadcast_to(codes_ref[...], codes_scratch.shape)
+        lane = lax.broadcasted_iota(jnp.int32, (rows, BLOCK_SNPS), 1)
+        seen = (codes_scratch[...] != first_block + lane).astype(jnp.float32).astype(jnp.bfloat16)
+        sums = rows_sum(seen, probes_ref[...])
+        counts = rows_sum(seen, jnp.ones((rows, BLOCK_SNPS), jnp.bfloat16))
+        out_ref[pl.ds(half + 2 * half_blocks, half_blocks)] = sums[:half_blocks]
+        out_ref[pl.ds(half + 3 * half_blocks, half_blocks)] = counts[:half_blocks]
+
+    for i in range(per_step):
+        block = step * per_step + i
+        seen = codes_scratch[...] != first_block + block
+        dosage = jnp.where(
+            seen, genotypes_ref[:, i * BLOCK_SNPS : (i + 1) * BLOCK_SNPS].astype(jnp.float32), 0.0
+        )
+        out_ref[pl.ds(pl.multiple_of(block * BLOCK_SNPS, BLOCK_SNPS), BLOCK_SNPS)] = rows_sum(
+            dosage.astype(jnp.bfloat16), probes_ref[...]
+        )
+        out_ref[pl.ds(half + block, 1)] = jnp.sum(dosage, 0, keepdims=True)
+        out_ref[pl.ds(half + half_blocks + block, 1)] = jnp.sum(dosage * dosage, 0, keepdims=True)
+
+
+def moments(which, genotypes, probes, codes):
+    rows, snps = genotypes.shape
+    half = snps // 2
+    steps = half // COLUMNS
+    return pl.pallas_call(
+        moments_kernel,
+        grid_spec=pltpu.PrefetchScalarGridSpec(
+            num_scalar_prefetch=1,
+            grid=(steps,),
+            in_specs=[
+                pl.BlockSpec((rows, COLUMNS), lambda i, h: (0, h[0] * steps + i)),
+                pl.BlockSpec(probes.shape, lambda i, h: (0, 0)),
+                pl.BlockSpec(codes.shape, lambda i, h: (0, 0)),
+            ],
+            out_specs=pl.BlockSpec((half + EXTRA, BLOCK_SNPS), lambda i, h: (0, 0)),
+            scratch_shapes=[pltpu.VMEM((rows, BLOCK_SNPS), jnp.int32)],
+        ),
+        out_shape=jax.ShapeDtypeStruct((half + EXTRA, BLOCK_SNPS), jnp.float32),
+        compiler_params=VMEM,
+        cost_estimate=pl.CostEstimate(
+            flops=1_500_000_000, bytes_accessed=3_000_000, transcendentals=0
+        ),
+    )(which.reshape(1), genotypes, probes, codes)
+
+
 def per_device(genotypes, probes, missing_codes):
     rows, snps = genotypes.shape
     probe_count = probes.shape[1]
     total_rows = rows * math.prod(lax.axis_size(a) for a in ALL)
     core = lax.axis_index("c")
-    blocks = snps // BLOCK_SNPS
     half = snps // 2
-    block_half = blocks // 2
     wide_x, wide_y = lax.axis_size("x"), lax.axis_size("y")
-
-    snp_block = jnp.arange(snps) // BLOCK_SNPS
-    seen = snp_block[None, :] != missing_codes[:, None]
-    observed = seen.astype(jnp.float32)
-    kept = jnp.where(seen, genotypes, jnp.zeros_like(genotypes))
-    dosage = kept.astype(jnp.float32)
-    raw = jnp.einsum("rs,rb->sb", kept, probes, preferred_element_type=jnp.float32)
-    total = jnp.sum(dosage, 0).reshape(blocks, BLOCK_SNPS)
-    square = jnp.sum(dosage * dosage, 0).reshape(blocks, BLOCK_SNPS)
-    by_block = jnp.arange(blocks)[None, :] != missing_codes[:, None]
-    seen_probes = jnp.einsum(
-        "rk,rb->kb", by_block.astype(jnp.bfloat16), probes, preferred_element_type=jnp.float32
-    )
-    count = jnp.broadcast_to(
-        jnp.sum(by_block.astype(jnp.float32), 0)[:, None], (blocks, BLOCK_SNPS)
-    )
-
-    def part(which):
-        def take(a):
-            n = a.shape[0] // 2
-            return lax.dynamic_slice_in_dim(a, which * n, n)
-
-        return jnp.concatenate([take(a) for a in (raw, total, square, seen_probes, count)])
-
-    mine = part(core) + swapped(part(1 - core))
+    codes = missing_codes.reshape(rows, 1)
+
+    sent = moments(1 - core, genotypes, probes, codes)
+    mine = moments(core, genotypes, probes, codes) + swapped(sent)
     mine = summed_parts(mine, "x")
     mine = summed_parts(mine, "y")
     mine = jnp.sum(copies(mine, "z"), 0)
@@ -159,6 +220,8 @@
     other = swapped(mine)
     first = jnp.where(core == 0, mine, other)
     second = jnp.where(core == 0, other, mine)
+    blocks = snps // BLOCK_SNPS
+    block_half = blocks // 2
 
     def joined(start, length):
         return jnp.concatenate([first[start : start + length], second[start : start + length]])
@@ -175,6 +238,8 @@
     )
     projection = (centred * inv_sd[:, :, None] / math.sqrt(total_rows)).astype(jnp.bfloat16)
     projection = projection.reshape(snps, probe_count)
+    snp_block = jnp.arange(snps) // BLOCK_SNPS
+    observed = (snp_block[None, :] != missing_codes[:, None]).astype(jnp.float32)
     standard = (
         (genotypes.astype(jnp.float32) - mean.reshape(1, snps)) * inv_sd.reshape(1, snps) * observed
     ).astype(jnp.bfloat16)

time: 170 us -> 173 us (1.018)
  Pallas kernels: 9.06 us -> 14.1 us
  other arithmetic: 5.35 us -> 2.58 us
  matrix products: 8.53 us -> 6.77 us
    pallas_call x0 -> x2, Pallas kernels: none -> 8.04 us  [moments(): pl.pallas_call(moments_kernel, grid_spec=pltpu.PrefetchScalarGridSpec(num...]
    reduce_sum x2 -> x0, other arithmetic: 3.82 us -> none  [the longest x1 3.69 us: per_device(): square = jnp.sum(dosage * dosage, 0).reshape(blocks, BLOCK_SNPS)]
    all_to_all x1, waiting for transfers between devices: 0.35 us -> 3.37 us  [exchanged(): return lax.all_to_all(blocks, axis, 0, 0, tiled=True)]
    pallas_call x1, Pallas kernels: 9.06 us -> 6.03 us  [inverse_of_factor(): pl.pallas_call(inverse_kernel, out_shape=jax.ShapeDtypeStruct((n, n), jnp...]
    dot_general x2 -> x0, matrix products: 1.78 us -> none  [the longest x1 1.63 us: per_device(): jnp.einsum('rs,rb->sb', kept, probes, preferred_element_type=jnp.float32)]
  transfers between devices with their start and end apart: 6 -> 6, of which waited for: 5 -> 4; matrix products, arithmetic and copies ran while one was open for 1% -> 1% of each run, Pallas kernels for 5% -> 6%
where the time goes in v4:
time: 173 us; the launch traced here: 172 us
  blocking collectives  106 us (61%)
  starting transfers between devices  32.2 us (19%)
  Pallas kernels  14.1 us (8%)
  waiting for transfers between devices  6.9 us (4%)
  matrix products  6.77 us (4%)
  local copies, waits for them, and re-layouts  2.89 us (2%)
  other arithmetic  2.58 us (1%)
    all_to_all x9, blocking collectives, exchanged(): return lax.all_to_all(blocks, axis, 0, 0, tiled=True)  106 us
    ppermute x5, starting transfers between devices, swapped(): return lax.ppermute(array, 'c', SWAP)  28.5 us
    pallas_call x2, Pallas kernels, moments(): pl.pallas_call(moments_kernel, grid_spec=pltpu.PrefetchScalarGridSpec(num...  8.04 us
    pallas_call x1, Pallas kernels, inverse_of_factor(): pl.pallas_call(inverse_kernel, out_shape=jax.ShapeDtypeStruct((n, n), jnp...  6.03 us
    all_to_all x1, starting transfers between devices, exchanged(): return lax.all_to_all(blocks, axis, 0, 0, tiled=True)  3.65 us
    ppermute x5, waiting for transfers between devices, swapped(): return lax.ppermute(array, 'c', SWAP)  3.53 us
  transfers between devices with their start and end apart: 6, of which 4 were waited for; matrix products, arithmetic and copies ran while one was open for 1% of the time, Pallas kernels for 6%

profile of v4, /device:TPU:1, one launch (start us, length us, event | category | flops | bytes accessed | tf_op | source)
XLA Modules:
  0.0 172.5 jit_solution(14874555716210726787)
XLA Ops:
  0.6 1.7 copy.9.codes_ref
  2.3 4.0 %shard_map.51 = f32[1056,128]{1,0:T(8,128)} custom-call(s32[1]{0:T(128)} %bitcast.2.half_ref, bf16[960,2048]{1,0:T(8,128)(2,1)} %genotypes_ref.3, bf16[960,128]{1,0:T(8,128)(2,1)} %probes_ref.3, s32[960,1]{1,0:T(8,128)} %copy.9.codes_ref), custom_call_target="tpu_custom_call" | custom-call | flops 1500000000 | bytes 3000000 | tf_op jit(solution)/shard_map/pallas_call | solution.py:183
  6.3 8.8 %collective-permute-start = (f32[1056,128]{1,0:T(8,128)}, f32[1056,128]{1,0:T(8,128)S(1)}, u32[]{:S(2)}, u32[]{:S(2)}) collective-permute-start(f32[1056,128]{1,0:T(8,128)} %shard_map.51), channel_id=1, source_target_pairs={{0,32},{32,0},{1,33},{33,1},{2,34},{34,2},{3,35},{35,3},{4,36},{36... | collective-permute-start | bytes 1622024 | tf_op jit(solution)/shard_map/ppermute | solution.py:31
  15.1 4.0 %shard_map.50 = f32[1056,128]{1,0:T(8,128)} custom-call(s32[1]{0:T(128)} %bitcast.half_ref.core_ref, bf16[960,2048]{1,0:T(8,128)(2,1)} %genotypes_ref.3, bf16[960,128]{1,0:T(8,128)(2,1)} %probes_ref.3, s32[960,1]{1,0:T(8,128)} %copy.9.codes_ref), custom_call_target="tpu_custom_call" | custom-call | flops 1500000000 | bytes 3000000 | tf_op jit(solution)/shard_map/pallas_call | solution.py:183
  19.1 0.0 collective-permute-done
  19.1 1.1 add.39
  20.3 12.2 %all_to_all.50 = f32[4,264,128]{2,1,0:T(8,128)S(1)} all-to-all(f32[4,264,128]{2,1,0:T(8,128)S(1)} %bitcast.62), channel_id=1, replica_groups=mesh['z'=8,'c'=2,'y'=8,'x'=4] {'x'}, dimensions={0} | all-to-all | bytes 1081344 | tf_op jit(solution)/shard_map/all_to_all | solution.py:17
  32.5 10.4 %all_to_all.51 = f32[8,33,128]{2,1,0:T(8,128)S(1)} all-to-all(f32[8,33,128]{2,1,0:T(8,128)S(1)} %reshape.156), channel_id=1, replica_groups=mesh['z'=8,'c'=2,'y'=8,'x'=4] {'y'}, dimensions={0} | all-to-all | bytes 270336 | tf_op jit(solution)/shard_map/all_to_all | solution.py:17
  43.0 18.4 %all_to_all.52 = f32[8,33,128]{2,1,0:T(8,128)S(1)} all-to-all(f32[8,33,128]{2,1,0:T(8,128)S(1)} %broadcast_in_dim.18), channel_id=1, replica_groups=mesh['z'=8,'c'=2,'y'=8,'x'=4] {'z'}, dimensions={0} | all-to-all | bytes 270336 | tf_op jit(solution)/shard_map/all_to_all | solution.py:17
  61.4 10.7 %all_to_all.53 = f32[8,33,128]{2,1,0:T(8,128)S(1)} all-to-all(f32[8,33,128]{2,1,0:T(8,128)S(1)} %broadcast_in_dim.19), channel_id=1, replica_groups=mesh['z'=8,'c'=2,'y'=8,'x'=4] {'y'}, dimensions={0} | all-to-all | bytes 270336 | tf_op jit(solution)/shard_map/all_to_all | solution.py:17
  72.1 0.0 copy-start
  72.1 9.4 %all_to_all.54 = f32[4,264,128]{2,1,0:T(8,128)S(1)} all-to-all(f32[4,264,128]{2,1,0:T(8,128)S(1)} %broadcast_in_dim.21), channel_id=1, replica_groups=mesh['z'=8,'c'=2,'y'=8,'x'=4] {'x'}, dimensions={0} | all-to-all | bytes 1081344 | tf_op jit(solution)/shard_map/all_to_all | solution.py:17
  81.5 8.1 %collective-permute-start.1 = (f32[1056,128]{1,0:T(8,128)S(1)}, f32[1056,128]{1,0:T(8,128)S(1)}, u32[]{:S(2)}, u32[]{:S(2)}) collective-permute-start(f32[1056,128]{1,0:T(8,128)S(1)} %bitcast.63), channel_id=1, source_target_pairs={{0,32},{32,0},{1,33},{33,1},{2,34},{34,2},{3,35},{35,3},{4,36},{36... | collective-permute-start | bytes 1622024 | tf_op jit(solution)/shard_map/ppermute | solution.py:31
  89.6 0.0 copy-start.1
  89.7 1.5 collective-permute-done.1
  91.2 0.1 broadcast_select_fusion.1
  91.5 1.1 fusion.5
  92.5 0.0 copy-done
  92.5 0.0 copy-done.1
  92.6 1.8 %fusion.2 = bf16[960,128]{1,0:T(8,128)(2,1)S(1)} fusion(bf16[2048,128]{1,0:T(8,128)(2,1)S(1)} %fusion.5, bf16[960,2048]{1,0:T(8,128)(2,1)S(1)} %copy-done.1, f32[2048]{0:T(1024)S(1)} %fusion.19, f32[2048]{0:T(1024)S(1)} %fusion.15, s32[2048]{0:T(1024)S(1)} %add_select_fusion, s32[960]{0:T(1024)S(1)} %copy-done), kind=kOutput, calls=%fused_computation.6 | convolution fusion | flops 515358720 | bytes 4730624 | tf_op jit(solution)/shard_map/dot_general | solution.py:247
  94.3 1.9 %fusion.12 = f32[2048,128]{1,0:T(8,128)S(1)} fusion(bf16[960,128]{1,0:T(8,128)(2,1)S(1)} %fusion.2, bf16[960,2048]{1,0:T(8,128)(2,1)S(1)} %copy-done.1, f32[2048]{0:T(1024)S(1)} %fusion.19, f32[2048]{0:T(1024)S(1)} %fusion.15, s32[2048]{0:T(1024)S(1)} %add_select_fusion, s32[960]{0:T(1024)S(1)} %copy-done), kind=kOutput, calls=%fused_computation.24 | convolution fusion | flops 515112960 | bytes 5254912 | tf_op jit(solution)/shard_map/rs,rb->sb/dot_general | solution.py:250
  96.2 0.3 fusion.31
  96.5 0.1 constant_dynamic-slice_fusion.3
  96.6 2.3 %collective-permute-start.2 = (f32[1088,128]{1,0:T(8,128)S(1)}, f32[1088,128]{1,0:T(8,128)S(1)}, u32[]{:S(2)}, u32[]{:S(2)}) collective-permute-start(f32[1088,128]{1,0:T(8,128)S(1)} %pad_maximum_fusion.1), channel_id=1, source_target_pairs={{0,32},{32,0},{1,33},{33,1},{2,34},{34,2},{3,35},{35,3},{4,36},{36... | collective-permute-start | bytes 1671176 | tf_op jit(solution)/shard_map/ppermute | solution.py:31
  98.9 1.6 collective-permute-done.2
  100.5 0.1 maximum_add_fusion
  100.7 13.0 %all_to_all.55 = f32[4,320,128]{2,1,0:T(8,128)S(1)} all-to-all(f32[4,320,128]{2,1,0:T(8,128)S(1)} %pad_maximum_fusion), channel_id=1, replica_groups=mesh['z'=8,'c'=2,'y'=8,'x'=4] {'x'}, dimensions={0} | all-to-all | bytes 1310720 | tf_op jit(solution)/shard_map/all_to_all | solution.py:17
  113.8 10.5 %all_to_all.56 = f32[8,40,128]{2,1,0:T(8,128)S(1)} all-to-all(f32[8,40,128]{2,1,0:T(8,128)S(1)} %pad_maximum_fusion.2), channel_id=1, replica_groups=mesh['z'=8,'c'=2,'y'=8,'x'=4] {'y'}, dimensions={0} | all-to-all | bytes 327680 | tf_op jit(solution)/shard_map/all_to_all | solution.py:17
  124.3 10.8 %all_to_all.57 = f32[8,40,128]{2,1,0:T(8,128)S(1)} all-to-all(f32[8,40,128]{2,1,0:T(8,128)S(1)} %broadcast_in_dim.23), channel_id=1, replica_groups=mesh['z'=8,'c'=2,'y'=8,'x'=4] {'z'}, dimensions={0} | all-to-all | bytes 327680 | tf_op jit(solution)/shard_map/all_to_all | solution.py:17
  135.1 10.8 %all_to_all.58 = f32[8,40,128]{2,1,0:T(8,128)S(1)} all-to-all(f32[8,40,128]{2,1,0:T(8,128)S(1)} %broadcast_in_dim.24), channel_id=1, replica_groups=mesh['z'=8,'c'=2,'y'=8,'x'=4] {'y'}, dimensions={0} | all-to-all | bytes 327680 | tf_op jit(solution)/shard_map/all_to_all | solution.py:17
  145.9 6.7 %collective-permute-start.3 = (f32[64,128]{1,0:T(8,128)S(1)}, f32[64,128]{1,0:T(8,128)S(1)}, u32[]{:S(2)}, u32[]{:S(2)}) collective-permute-start(f32[64,128]{1,0:T(8,128)S(1)} %slice_bitcast_fusion.near_ref), channel_id=1, source_target_pairs={{0,32},{32,0},{1,33},{33,1},{2,34},{34,2},{3,35},{35,3},{4,36},{36... | collective-permute-start | bytes 98312 | tf_op jit(solution)/shard_map/ppermute | solution.py:31
  152.6 0.8 broadcast_in_dim.26
  153.4 3.7 %all-to-all-start.9 = ((f32[4,256,128]{2,1,0:T(8,128)}), f32[4,256,128]{2,1,0:T(8,128)S(1)}, u32[]{:S(2)}, u32[]{:S(2)}) async-start(f32[4,256,128]{2,1,0:T(8,128)} %broadcast_in_dim.26), calls=%async_computation.9 | async-start | bytes 1048576 | tf_op jit(solution)/shard_map/all_to_all | solution.py:17
  157.0 0.0 collective-permute-done.3.far_ref
  157.1 6.0 %shard_map.52 = f32[128,128]{1,0:T(8,128)S(1)} custom-call(f32[64,128]{1,0:T(8,128)S(1)} %slice_bitcast_fusion.near_ref, f32[64,128]{1,0:T(8,128)S(1)} %collective-permute-done.3.far_ref, s32[1]{0:T(128)} %bitcast.half_ref.core_ref), custom_call_target="tpu_custom_call" | custom-call | flops 8999999488 | bytes 1000000 | tf_op jit(solution)/shard_map/pallas_call | solution.py:123
  163.1 3.4 %all-to-all-done.9 = f32[4,256,128]{2,1,0:T(8,128)S(1)} async-done(((f32[4,256,128]{2,1,0:T(8,128)}), f32[4,256,128]{2,1,0:T(8,128)S(1)}, u32[]{:S(2)}, u32[]{:S(2)}) %all-to-all-start.9) | async-done | bytes 524320 | tf_op jit(solution)/shard_map/all_to_all | solution.py:17
  166.5 2.7 %collective-permute-start.4 = (f32[1024,128]{1,0:T(8,128)S(1)}, f32[1024,128]{1,0:T(8,128)S(1)}, u32[]{:S(2)}, u32[]{:S(2)}) collective-permute-start(f32[1024,128]{1,0:T(8,128)S(1)} %bitcast.66), channel_id=1, source_target_pairs={{0,32},{32,0},{1,33},{33,1},{2,34},{34,2},{3,35},{35,3},{4,36},{36... | collective-permute-start | bytes 1572872 | tf_op jit(solution)/shard_map/ppermute | solution.py:31
  169.2 1.1 fusion.1
  170.2 0.4 collective-permute-done.4
  170.7 1.8 %fusion = bf16[2048,128]{1,0:T(8,128)(2,1)} fusion(f32[128,128]{1,0:T(8,128)S(1)} %shard_map.52, f32[1024,128]{1,0:T(8,128)S(1)} %collective-permute-done.4, f32[1024,128]{1,0:T(8,128)S(1)} %bitcast.67, pred[]{:T(512)S(6)} %eq.2), kind=kOutput, calls=%fused_computation.2 | convolution fusion | flops 403963904 | bytes 1638401 | tf_op jit(solution)/shard_map/dot_general | solution.py:296
  (33 shorter events, 0.6 us)
Async XLA Ops:
  6.3 12.8 %collective-permute-start = (f32[1056,128]{1,0:T(8,128)}, f32[1056,128]{1,0:T(8,128)S(1)}, u32[]{:S(2)}, u32[]{:S(2)}) collective-permute-start(f32[1056,128]{1,0:T(8,128)} %shard_map.51), channel_id=1, source_target_pairs={{0,32},{32,0},{1,33},{33,1},{2,34},{34,2},{3,35},{35,3},{4,36},{36... | collective-permute-start | bytes 1622024 | tf_op jit(solution)/shard_map/ppermute | solution.py:31
  72.1 20.5 %copy-start = (s32[960]{0:T(1024)S(1)}, s32[960]{0:T(1024)}, u32[]{:S(2)}) copy-start(s32[960]{0:T(1024)} %param.5) | copy-start | bytes 11524
  81.5 9.7 %collective-permute-start.1 = (f32[1056,128]{1,0:T(8,128)S(1)}, f32[1056,128]{1,0:T(8,128)S(1)}, u32[]{:S(2)}, u32[]{:S(2)}) collective-permute-start(f32[1056,128]{1,0:T(8,128)S(1)} %bitcast.63), channel_id=1, source_target_pairs={{0,32},{32,0},{1,33},{33,1},{2,34},{34,2},{3,35},{35,3},{4,36},{36... | collective-permute-start | bytes 1622024 | tf_op jit(solution)/shard_map/ppermute | solution.py:31
  89.6 2.9 %copy-start.1 = (bf16[960,2048]{1,0:T(8,128)(2,1)S(1)}, bf16[960,2048]{1,0:T(8,128)(2,1)}, u32[]{:S(2)}) copy-start(bf16[960,2048]{1,0:T(8,128)(2,1)} %genotypes_ref.3) | copy-start | bytes 11796484
  96.6 3.9 %collective-permute-start.2 = (f32[1088,128]{1,0:T(8,128)S(1)}, f32[1088,128]{1,0:T(8,128)S(1)}, u32[]{:S(2)}, u32[]{:S(2)}) collective-permute-start(f32[1088,128]{1,0:T(8,128)S(1)} %pad_maximum_fusion.1), channel_id=1, source_target_pairs={{0,32},{32,0},{1,33},{33,1},{2,34},{34,2},{3,35},{35,3},{4,36},{36... | collective-permute-start | bytes 1671176 | tf_op jit(solution)/shard_map/ppermute | solution.py:31
  145.9 11.2 %collective-permute-start.3 = (f32[64,128]{1,0:T(8,128)S(1)}, f32[64,128]{1,0:T(8,128)S(1)}, u32[]{:S(2)}, u32[]{:S(2)}) collective-permute-start(f32[64,128]{1,0:T(8,128)S(1)} %slice_bitcast_fusion.near_ref), channel_id=1, source_target_pairs={{0,32},{32,0},{1,33},{33,1},{2,34},{34,2},{3,35},{35,3},{4,36},{36... | collective-permute-start | bytes 98312 | tf_op jit(solution)/shard_map/ppermute | solution.py:31
  153.4 13.1 %all-to-all-start.9 = ((f32[4,256,128]{2,1,0:T(8,128)}), f32[4,256,128]{2,1,0:T(8,128)S(1)}, u32[]{:S(2)}, u32[]{:S(2)}) async-start(f32[4,256,128]{2,1,0:T(8,128)} %broadcast_in_dim.26), calls=%async_computation.9 | async-start | bytes 1048576 | tf_op jit(solution)/shard_map/all_to_all | solution.py:17
  166.5 4.2 %collective-permute-start.4 = (f32[1024,128]{1,0:T(8,128)S(1)}, f32[1024,128]{1,0:T(8,128)S(1)}, u32[]{:S(2)}, u32[]{:S(2)}) collective-permute-start(f32[1024,128]{1,0:T(8,128)S(1)} %bitcast.66), channel_id=1, source_target_pairs={{0,32},{32,0},{1,33},{33,1},{2,34},{34,2},{3,35},{35,3},{4,36},{36... | collective-permute-start | bytes 1572872 | tf_op jit(solution)/shard_map/ppermute | solution.py:31

commit v5 on v1

v5 whole, which is shorter than its diff:
```python
import math

import jax
import jax.numpy as jnp
from jax import lax
from jax.experimental import pallas as pl
from jax.experimental.pallas import tpu as pltpu
from jax.sharding import Mesh
from jax.sharding import PartitionSpec as P

BLOCK_SNPS = 128
ALL = ("z", "c", "y", "x")
SWAP = ((0, 1), (1, 0))


def exchanged(blocks, axis):
    return lax.all_to_all(blocks, axis, 0, 0, tiled=True)


def flat_sum(array, axis):
    blocks = array.reshape(lax.axis_size(axis), 1, -1)
    return jnp.sum(exchanged(blocks, axis), 0)


def flat_copies(flat, axis):
    return exchanged(jnp.broadcast_to(flat[None], (lax.axis_size(axis), *flat.shape)), axis)


def summed_everywhere(array):
    shard = flat_sum(array, ("y", "x"))
    shard = jnp.sum(flat_copies(shard, "z"), 0)
    return flat_copies(shard, ("y", "x")).reshape(array.shape)


def swapped(array):
    return lax.ppermute(array, "c", SWAP)

def panel(upper, under, base, extra):
    step, n = upper.shape
    row_of = lax.broadcasted_iota(jnp.int32, (step, n), 0)
    a = [
        [
            jnp.broadcast_to(upper[i : i + 1, base + k : base + k + 1], (step, n))
            if k >= i
            else None
            for k in range(step)
        ]
        for i in range(step)
    ]
    x = [[None] * step for _ in range(step)]
    scale = []
    for t in range(step):
        r = lax.rsqrt(a[t][t])
        scale.append(r)
        u = [None] * step
        for k in range(t + 1, step):
            u[k] = a[t][k] * r
        for i in range(t + 1, step):
            for k in range(i, step):
                a[i][k] = a[i][k] - u[i] * u[k]
        a[t] = u
    for i in range(step):
        x[i][i] = scale[i]
        for k in range(i):
            s = a[k][i] * x[k][k]
            for m in range(k + 1, i):
                s = s + a[m][i] * x[m][k]
            x[i][k] = -s * scale[i]
    both = jnp.concatenate([upper, under], 1)
    out = None
    for k in range(step):
        col = jnp.zeros((step, n), jnp.float32)
        for i in range(k, step):
            col = jnp.where(row_of == i, x[i][k], col)
        term = jnp.concatenate([col, col], 1) * both[k : k + 1]
        out = term if out is None else out + term
    columns = None
    if extra is not None:
        raw = [jnp.broadcast_to(extra[:, base + k : base + k + 1], (step, n)) for k in range(step)]
        columns = []
        for t in range(step):
            s = raw[0] * x[t][0]
            for k in range(1, t + 1):
                s = s + raw[k] * x[t][k]
            columns.append(s)
    return out, columns


def inverse_factor(gram):
    n = gram.shape[0]
    step = 8
    left = gram
    inv = (
        lax.broadcasted_iota(jnp.int32, (n, n), 0) == lax.broadcasted_iota(jnp.int32, (n, n), 1)
    ).astype(jnp.float32)
    done = []
    for base in range(0, n, 2 * step):
        first, columns = panel(left[:step], inv[:step], base, left[step : 2 * step])
        both = jnp.concatenate([left[step : 2 * step], inv[step : 2 * step]], 1)
        for t in range(step):
            both = both - jnp.concatenate([columns[t], columns[t]], 1) * first[t : t + 1]
        second, _ = panel(both[:, :n], both[:, n:], base + step, None)
        out = jnp.concatenate([first, second], 0)
        done.append(out[:, n:])
        if base + 2 * step < n:
            prod = lax.dot_general(
                out[:, :n],
                out,
                (((0,), (0,)), ((), ())),
                precision=lax.Precision.HIGHEST,
                preferred_element_type=jnp.float32,
            )
            left = left[2 * step :] - prod[base + 2 * step :, :n]
            inv = inv[2 * step :] - prod[base + 2 * step :, n:]
    return jnp.concatenate(done, 0)


def inverse_kernel(scale, first_ref, second_ref, inverse_ref):
    gram = first_ref[...] + second_ref[...]
    inverse_ref[...] = inverse_factor((gram + gram.T) * (0.5 * scale))


def inverse_of_factor(scale, first, second):
    return pl.pallas_call(
        lambda *refs: inverse_kernel(scale, *refs),
        out_shape=jax.ShapeDtypeStruct(first.shape, jnp.float32),
        in_specs=[pl.BlockSpec(memory_space=pltpu.VMEM)] * 2,
        out_specs=pl.BlockSpec(memory_space=pltpu.VMEM),
        compiler_params=pltpu.CompilerParams(vmem_limit_bytes=32 * 2**20),
        cost_estimate=pl.CostEstimate(
            flops=6_000_000_000, bytes_accessed=1_000_000, transcendentals=128
        ),
    )(first, second)


def per_device(genotypes, probes, missing_codes):
    rows, snps = genotypes.shape
    probe_count = probes.shape[1]
    total_rows = rows * math.prod(lax.axis_size(a) for a in ALL)
    core = lax.axis_index("c")
    blocks = snps // BLOCK_SNPS
    half = snps // 2
    block_half = blocks // 2

    snp_block = jnp.arange(snps) // BLOCK_SNPS
    seen = snp_block[None, :] != missing_codes[:, None]
    observed = seen.astype(jnp.float32)
    kept = jnp.where(seen, genotypes, jnp.zeros_like(genotypes))
    dosage = kept.astype(jnp.float32)
    raw = jnp.einsum("rs,rb->sb", kept, probes, preferred_element_type=jnp.float32)
    total = jnp.sum(dosage, 0).reshape(blocks, BLOCK_SNPS)
    square = jnp.sum(dosage * dosage, 0).reshape(blocks, BLOCK_SNPS)
    by_block = jnp.arange(blocks)[None, :] != missing_codes[:, None]
    seen_probes = jnp.einsum(
        "rk,rb->kb", by_block.astype(jnp.bfloat16), probes, preferred_element_type=jnp.float32
    )
    count = jnp.broadcast_to(
        jnp.sum(by_block.astype(jnp.float32), 0)[:, None], (blocks, BLOCK_SNPS)
    )

    def part(which):
        def take(a):
            n = a.shape[0] // 2
            return lax.dynamic_slice_in_dim(a, which * n, n)

        return jnp.concatenate([take(a) for a in (raw, total, square, seen_probes, count)])

    mine = part(core) + swapped(part(1 - core))
    mine = summed_everywhere(mine)
    other = swapped(mine)
    first = jnp.where(core == 0, mine, other)
    second = jnp.where(core == 0, other, mine)

    def joined(start, length):
        return jnp.concatenate([first[start : start + length], second[start : start + length]])

    raw = joined(0, half)
    total, square, seen_probes, count = (
        joined(half + i * block_half, block_half) for i in range(4)
    )
    counted = jnp.maximum(count, 1.0)
    mean = total / counted
    inv_sd = 1.0 / jnp.sqrt(square / counted - mean * mean + 1e-05)
    centred = (
        raw.reshape(blocks, BLOCK_SNPS, probe_count) - mean[:, :, None] * seen_probes[:, None, :]
    )
    projection = (centred * inv_sd[:, :, None] / math.sqrt(total_rows)).astype(jnp.bfloat16)
    projection = projection.reshape(snps, probe_count)
    standard = (
        (genotypes.astype(jnp.float32) - mean.reshape(1, snps)) * inv_sd.reshape(1, snps) * observed
    ).astype(jnp.bfloat16)
    image = (
        jnp.dot(standard, projection, preferred_element_type=jnp.float32) / math.sqrt(snps)
    ).astype(jnp.bfloat16)
    cross = jnp.einsum("rs,rb->sb", standard, image, preferred_element_type=jnp.float32)

    def part_of(array, which):
        return lax.dynamic_slice_in_dim(array, which * half, half)

    mine = part_of(cross, core) + swapped(part_of(cross, 1 - core))
    mine = summed_everywhere(mine)
    other = swapped(mine)

    def gram_of(which, cross_half):
        return jnp.einsum(
            "sb,sc->bc",
            part_of(projection, which).astype(jnp.float32),
            cross_half,
            precision=lax.Precision.HIGHEST,
        )

    inverse = inverse_of_factor(
        1.0 / math.sqrt(snps), gram_of(core, mine), gram_of(1 - core, other)
    )
    basis = jnp.dot(image.astype(jnp.float32), inverse.T, precision=lax.Precision.HIGHEST)
    cross = jnp.where(
        core == 0, jnp.concatenate([mine, other]), jnp.concatenate([other, mine])
    )
    scores = jnp.dot(cross, inverse.T, precision=lax.Precision.HIGHEST)
    return (
        (basis * math.sqrt(total_rows)).astype(jnp.bfloat16),
        (scores * math.sqrt(snps / total_rows)).astype(jnp.bfloat16),
    )


def solution(mesh):
    finer = Mesh(mesh.devices.reshape(8, 2, 8, 4), ALL)
    spec = (P(ALL, None), P(ALL, None), P(ALL))
    return jax.shard_map(
        per_device, mesh=finer, in_specs=spec, out_specs=(P(ALL, None), P()), check_vma=False
    )
```

time: 183 us -> 163 us (0.89)
  other arithmetic: 28.3 us -> 6.55 us
  Pallas kernels: 0 us -> 6.03 us
  starting transfers between devices: 31.8 us -> 25.8 us
    another operation x5 -> x0, other arithmetic: 22.9 us -> none  [the longest x3 12.4 us: per_device(): lower = jnp.linalg.cholesky(gram)]
    pallas_call x0 -> x1, Pallas kernels: none -> 6.03 us  [inverse_of_factor(): pl.pallas_call(lambda *refs: inverse_kernel(scale, *refs), out_shape=jax....]
    all_to_all x1 -> x0, starting transfers between devices: 3.65 us -> none  [exchanged(): return lax.all_to_all(blocks, axis, 0, 0, tiled=True)]
    ppermute x5 -> x4, starting transfers between devices: 28.1 us -> 25.8 us  [swapped(): return lax.ppermute(array, 'c', SWAP)]
    all_to_all x9 -> x6, blocking collectives: 106 us -> 107 us  [exchanged(): return lax.all_to_all(blocks, axis, 0, 0, tiled=True)]
    ppermute x5 -> x4, waiting for transfers between devices: 4.56 us -> 5.39 us  [swapped(): return lax.ppermute(array, 'c', SWAP)]
  transfers between devices with their start and end apart: 6 -> 4, of which waited for: 3 -> 4; matrix products, arithmetic and copies ran while one was open for 14% -> 0% of each run, Pallas kernels for 0% -> 0%
where the time goes in v5:
time: 163 us
  blocking collectives  107 us (66%)
  starting transfers between devices  25.8 us (16%)
  matrix products  10.2 us (6%)
  other arithmetic  6.55 us (4%)
  Pallas kernels  6.03 us (4%)
  waiting for transfers between devices  5.39 us (3%)
    all_to_all x6, blocking collectives, exchanged(): return lax.all_to_all(blocks, axis, 0, 0, tiled=True)  107 us
    ppermute x4, starting transfers between devices, swapped(): return lax.ppermute(array, 'c', SWAP)  25.8 us
    pallas_call x1, Pallas kernels, inverse_of_factor(): pl.pallas_call(lambda *refs: inverse_kernel(scale, *refs), out_shape=jax....  6.03 us
    ppermute x4, waiting for transfers between devices, swapped(): return lax.ppermute(array, 'c', SWAP)  5.39 us
    reduce_sum x1, other arithmetic, per_device(): square = jnp.sum(dosage * dosage, 0).reshape(blocks, BLOCK_SNPS)  3.41 us
  transfers between devices with their start and end apart: 4, of which 4 were waited for; matrix products, arithmetic and copies ran while one was open for 0% of the time, Pallas kernels for 0%

profile of v5, /device:TPU:1, one launch (start us, length us, event | category | flops | bytes accessed | tf_op | source)
XLA Modules:
  0.0 163.0 jit_solution(14257866445520908514)
XLA Ops:
  0.6 0.0 copy-start
  0.6 0.0 copy-start.3
  0.7 0.0 copy-start.1
  0.7 1.0 convert_reduce_fusion.1
  1.6 0.0 copy-done
  1.7 1.1 fusion.21
  2.8 3.4 %fusion = (f32[2048]{0:T(1024)S(1)}, f32[2048]{0:T(1024)S(1)}) fusion(bf16[960,2048]{1,0:T(8,128)(2,1)} %param.3, s32[960]{0:T(1024)} %param.5, s32[2048]{0:T(1024)S(1)} %add_select_fusion), kind=kLoop, calls=%fused_computation.4 | loop fusion | flops 11792384 | bytes 3960576 | tf_op jit(solution)/shard_map/reduce_sum | solution.py:152
  6.2 0.0 copy-done.3
  6.2 0.0 copy-done.1
  6.2 1.6 fusion.41
  7.9 0.1 fusion.44
  7.9 0.1 dynamic-slice_dynamic-update-slice_fusion
  8.1 0.1 constant_dynamic-update-slice_fusion.4
  8.2 8.8 %collective-permute-start = (f32[1056,128]{1,0:T(8,128)S(1)}, f32[1056,128]{1,0:T(8,128)S(1)}, u32[]{:S(2)}, u32[]{:S(2)}) collective-permute-start(f32[1056,128]{1,0:T(8,128)S(1)} %constant_dynamic-update-slice_fusion.4), channel_id=1, source_target_pairs={{0,32},{32,0},{1,33},{33,1},{2,34},{34,2},{3,35},{35,3},{4,36},{36... | collective-permute-start | bytes 1622024 | tf_op jit(solution)/shard_map/ppermute | solution.py:36
  16.9 0.1 constant_dynamic-update-slice_fusion
  17.0 1.5 collective-permute-done
  18.5 0.1 add.53
  18.5 20.9 %all_to_all.30 = f32[32,1,4224]{2,1,0:T(1,128)S(1)} all-to-all(f32[32,1,4224]{2,1,0:T(1,128)S(1)} %bitcast.55), channel_id=1, replica_groups=mesh['z'=8,'c'=2,'y'=8,'x'=4] {'y','x'}, dimensions={0} | all-to-all | bytes 1081344 | tf_op jit(solution)/shard_map/all_to_all | solution.py:17
  39.5 0.3 reduce_sum.66
  39.8 0.1 broadcast_in_dim.17
  39.9 17.9 %all_to_all.31 = f32[8,1,4224]{2,1,0:T(1,128)S(1)} all-to-all(f32[8,1,4224]{2,1,0:T(1,128)S(1)} %broadcast_in_dim.17), channel_id=1, replica_groups=mesh['z'=8,'c'=2,'y'=8,'x'=4] {'z'}, dimensions={0} | all-to-all | bytes 270336 | tf_op jit(solution)/shard_map/all_to_all | solution.py:17
  57.8 0.1 reduce_sum.67
  57.9 0.3 broadcast_in_dim.18
  58.2 18.4 %all_to_all.32 = f32[32,1,4224]{2,1,0:T(1,128)S(1)} all-to-all(f32[32,1,4224]{2,1,0:T(1,128)S(1)} %broadcast_in_dim.18), channel_id=1, replica_groups=mesh['z'=8,'c'=2,'y'=8,'x'=4] {'y','x'}, dimensions={0} | all-to-all | bytes 1081344 | tf_op jit(solution)/shard_map/all_to_all | solution.py:17
  76.5 7.5 %collective-permute-start.1 = (f32[1056,128]{1,0:T(8,128)S(1)}, f32[1056,128]{1,0:T(8,128)S(1)}, u32[]{:S(2)}, u32[]{:S(2)}) collective-permute-start(f32[1056,128]{1,0:T(8,128)S(1)} %bitcast.56), channel_id=1, source_target_pairs={{0,32},{32,0},{1,33},{33,1},{2,34},{34,2},{3,35},{35,3},{4,36},{36... | collective-permute-start | bytes 1622024 | tf_op jit(solution)/shard_map/ppermute | solution.py:36
  84.1 0.0 copy-start.2
  84.1 1.5 collective-permute-done.1
  85.6 0.1 broadcast_select_fusion.1
  85.9 1.1 fusion.7
  87.0 0.0 copy-done.2
  87.0 1.8 %fusion.4 = bf16[960,128]{1,0:T(8,128)(2,1)S(1)} fusion(bf16[2048,128]{1,0:T(8,128)(2,1)S(1)} %fusion.7, bf16[960,2048]{1,0:T(8,128)(2,1)S(1)} %copy-done.2, f32[2048]{0:T(1024)S(1)} %fusion.29, f32[2048]{0:T(1024)S(1)} %fusion.25, s32[2048]{0:T(1024)S(1)} %add_select_fusion, s32[960]{0:T(1024)S(1)} %copy-done.3), kind=kOutput, calls=%fused_computation.11 | convolution fusion | flops 515358720 | bytes 4730624 | tf_op jit(solution)/shard_map/dot_general | solution.py:193
  88.7 1.9 %fusion.18 = f32[2048,128]{1,0:T(8,128)S(1)} fusion(bf16[960,128]{1,0:T(8,128)(2,1)S(1)} %fusion.4, bf16[960,2048]{1,0:T(8,128)(2,1)S(1)} %copy-done.2, f32[2048]{0:T(1024)S(1)} %fusion.29, f32[2048]{0:T(1024)S(1)} %fusion.25, s32[2048]{0:T(1024)S(1)} %add_select_fusion, s32[960]{0:T(1024)S(1)} %copy-done.3), kind=kOutput, calls=%fused_computation.33 | convolution fusion | flops 515112960 | bytes 5254912 | tf_op jit(solution)/shard_map/rs,rb->sb/dot_general | solution.py:195
  90.7 2.3 %collective-permute-start.2 = (f32[1024,128]{1,0:T(8,128)S(1)}, f32[1024,128]{1,0:T(8,128)S(1)}, u32[]{:S(2)}, u32[]{:S(2)}) collective-permute-start(f32[1024,128]{1,0:T(8,128)S(1)} %constant_dynamic-slice_fusion), channel_id=1, source_target_pairs={{0,32},{32,0},{1,33},{33,1},{2,34},{34,2},{3,35},{35,3},{4,36},{36... | collective-permute-start | bytes 1572872 | tf_op jit(solution)/shard_map/ppermute | solution.py:36
  93.0 1.5 collective-permute-done.2
  94.5 0.1 dynamic-slice_add_fusion
  94.5 20.5 %all_to_all.33 = f32[32,1,4096]{2,1,0:T(1,128)S(1)} all-to-all(f32[32,1,4096]{2,1,0:T(1,128)S(1)} %bitcast.61), channel_id=1, replica_groups=mesh['z'=8,'c'=2,'y'=8,'x'=4] {'y','x'}, dimensions={0} | all-to-all | bytes 1048576 | tf_op jit(solution)/shard_map/all_to_all | solution.py:17
  115.0 0.4 reduce_sum.68
  115.4 0.1 broadcast_in_dim.19
  115.5 10.4 %all_to_all.34 = f32[8,1,4096]{2,1,0:T(1,128)S(1)} all-to-all(f32[8,1,4096]{2,1,0:T(1,128)S(1)} %broadcast_in_dim.19), channel_id=1, replica_groups=mesh['z'=8,'c'=2,'y'=8,'x'=4] {'z'}, dimensions={0} | all-to-all | bytes 262144 | tf_op jit(solution)/shard_map/all_to_all | solution.py:17
  125.9 0.1 reduce_sum.69
  126.0 0.5 broadcast_in_dim.20
  126.5 18.7 %all_to_all.35 = f32[32,1,4096]{2,1,0:T(1,128)S(1)} all-to-all(f32[32,1,4096]{2,1,0:T(1,128)S(1)} %broadcast_in_dim.20), channel_id=1, replica_groups=mesh['z'=8,'c'=2,'y'=8,'x'=4] {'y','x'}, dimensions={0} | all-to-all | bytes 1048576 | tf_op jit(solution)/shard_map/all_to_all | solution.py:17
  145.1 7.2 %collective-permute-start.3 = (f32[1024,128]{1,0:T(8,128)S(1)}, f32[1024,128]{1,0:T(8,128)S(1)}, u32[]{:S(2)}, u32[]{:S(2)}) collective-permute-start(f32[1024,128]{1,0:T(8,128)S(1)} %bitcast.58), channel_id=1, source_target_pairs={{0,32},{32,0},{1,33},{33,1},{2,34},{34,2},{3,35},{35,3},{4,36},{36... | collective-permute-start | bytes 1572872 | tf_op jit(solution)/shard_map/ppermute | solution.py:36
  152.3 0.4 fusion.16.refs_0_
  152.8 0.9 collective-permute-done.3
  153.7 0.4 fusion.14.refs_1_
  154.1 6.0 %shard_map.50 = f32[128,128]{1,0:T(8,128)S(1)} custom-call(f32[128,128]{1,0:T(8,128)S(1)} %fusion.16.refs_0_, f32[128,128]{1,0:T(8,128)S(1)} %fusion.14.refs_1_), custom_call_target="tpu_custom_call" | custom-call | flops 6000000000 | bytes 1000000 | tf_op jit(solution)/shard_map/pallas_call | solution.py:124
  160.1 1.1 fusion.3
  161.2 1.8 %fusion.2 = bf16[2048,128]{1,0:T(8,128)(2,1)} fusion(f32[128,128]{1,0:T(8,128)S(1)} %shard_map.50, f32[1024,128]{1,0:T(8,128)S(1)} %collective-permute-done.3, f32[1024,128]{1,0:T(8,128)S(1)} %bitcast.60, pred[]{:T(512)S(6)} %eq.2), kind=kOutput, calls=%fused_computation.7 | convolution fusion | flops 403963904 | bytes 1638401 | tf_op jit(solution)/shard_map/dot_general | solution.py:219
  (13 shorter events, 0.2 us)
Async XLA Ops:
  0.6 1.0 copy-start
  0.6 5.6 %copy-start.3 = (s32[960]{0:T(1024)S(1)}, s32[960]{0:T(1024)}, u32[]{:S(2)}) copy-start(s32[960]{0:T(1024)} %param.5) | copy-start | bytes 11524
  0.7 5.6 %copy-start.1 = (bf16[960,2048]{1,0:T(8,128)(2,1)S(1)}, bf16[960,2048]{1,0:T(8,128)(2,1)}, u32[]{:S(2)}) copy-start(bf16[960,2048]{1,0:T(8,128)(2,1)} %param.3) | copy-start | bytes 11796484
  8.2 10.3 %collective-permute-start = (f32[1056,128]{1,0:T(8,128)S(1)}, f32[1056,128]{1,0:T(8,128)S(1)}, u32[]{:S(2)}, u32[]{:S(2)}) collective-permute-start(f32[1056,128]{1,0:T(8,128)S(1)} %constant_dynamic-update-slice_fusion.4), channel_id=1, source_target_pairs={{0,32},{32,0},{1,33},{33,1},{2,34},{34,2},{3,35},{35,3},{4,36},{36... | collective-permute-start | bytes 1622024 | tf_op jit(solution)/shard_map/ppermute | solution.py:36
  76.5 9.1 %collective-permute-start.1 = (f32[1056,128]{1,0:T(8,128)S(1)}, f32[1056,128]{1,0:T(8,128)S(1)}, u32[]{:S(2)}, u32[]{:S(2)}) collective-permute-start(f32[1056,128]{1,0:T(8,128)S(1)} %bitcast.56), channel_id=1, source_target_pairs={{0,32},{32,0},{1,33},{33,1},{2,34},{34,2},{3,35},{35,3},{4,36},{36... | collective-permute-start | bytes 1622024 | tf_op jit(solution)/shard_map/ppermute | solution.py:36
  84.1 2.9 %copy-start.2 = (bf16[960,2048]{1,0:T(8,128)(2,1)S(1)}, bf16[960,2048]{1,0:T(8,128)(2,1)}, u32[]{:S(2)}) copy-start(bf16[960,2048]{1,0:T(8,128)(2,1)} %param.3) | copy-start | bytes 11796484
  90.7 3.8 %collective-permute-start.2 = (f32[1024,128]{1,0:T(8,128)S(1)}, f32[1024,128]{1,0:T(8,128)S(1)}, u32[]{:S(2)}, u32[]{:S(2)}) collective-permute-start(f32[1024,128]{1,0:T(8,128)S(1)} %constant_dynamic-slice_fusion), channel_id=1, source_target_pairs={{0,32},{32,0},{1,33},{33,1},{2,34},{34,2},{3,35},{35,3},{4,36},{36... | collective-permute-start | bytes 1572872 | tf_op jit(solution)/shard_map/ppermute | solution.py:36
  145.1 8.5 %collective-permute-start.3 = (f32[1024,128]{1,0:T(8,128)S(1)}, f32[1024,128]{1,0:T(8,128)S(1)}, u32[]{:S(2)}, u32[]{:S(2)}) collective-permute-start(f32[1024,128]{1,0:T(8,128)S(1)} %bitcast.58), channel_id=1, source_target_pairs={{0,32},{32,0},{1,33},{33,1},{2,34},{34,2},{3,35},{35,3},{4,36},{36... | collective-permute-start | bytes 1572872 | tf_op jit(solution)/shard_map/ppermute | solution.py:36

commit v6 on v5

--- a/solution.py
+++ b/solution.py
@@ -17,19 +17,22 @@
     return lax.all_to_all(blocks, axis, 0, 0, tiled=True)
 
 
-def flat_sum(array, axis):
-    blocks = array.reshape(lax.axis_size(axis), 1, -1)
-    return jnp.sum(exchanged(blocks, axis), 0)
-
-
-def flat_copies(flat, axis):
-    return exchanged(jnp.broadcast_to(flat[None], (lax.axis_size(axis), *flat.shape)), axis)
+def blocks_of(array, size):
+    rows = array.shape[0] // size
+    if rows % 8:
+        return array.reshape(size, 1, rows * array.shape[1])
+    return array.reshape(size, rows, array.shape[1])
+
+
+def copies(shard, axis):
+    return exchanged(jnp.broadcast_to(shard[None], (lax.axis_size(axis), *shard.shape)), axis)
 
 
 def summed_everywhere(array):
-    shard = flat_sum(array, ("y", "x"))
-    shard = jnp.sum(flat_copies(shard, "z"), 0)
-    return flat_copies(shard, ("y", "x")).reshape(array.shape)
+    near = ("y", "x")
+    shard = jnp.sum(exchanged(blocks_of(array, lax.axis_size(near)), near), 0)
+    shard = jnp.sum(copies(shard, "z"), 0)
+    return copies(shard, near).reshape(array.shape)
 
 
 def swapped(array):
@@ -133,6 +136,109 @@
     )(first, second)
 
 
+EXTRA = 32
+CHUNK = 2 * BLOCK_SNPS
+PADDED = 128
+PIECES = 4
+
+
+def padded_rows(array, rows):
+    spare = rows - array.shape[0]
+    if not spare:
+        return array
+    return jnp.concatenate([array, jnp.zeros((spare, array.shape[1]), array.dtype)], 0)
+
+
+def moments_kernel(
+    which_ref, genotypes_ref, probes_ref, codes_ref, out_ref, held, turned, code_down, semaphores
+):
+    rows, probe_count = probes_ref.shape
+    half = held.shape[1]
+    chunks = half // CHUNK
+    half_blocks = half // BLOCK_SNPS
+    which = which_ref[0]
+    start = pl.multiple_of(which * half, half)
+    copies_in = []
+    pieces = semaphores.shape[0]
+    length = rows // pieces
+    for i in range(pieces):
+        at = pl.ds(i * length, length)
+        copy = pltpu.make_async_copy(
+            genotypes_ref.at[at, pl.ds(start, half)], held.at[at], semaphores.at[i]
+        )
+        copy.start()
+        copies_in.append(copy)
+
+    long = turned.shape[1]
+    probes = probes_ref[...]
+    turned[pl.ds(0, probe_count)] = (
+        padded_rows(probes.astype(jnp.float32), long).T.astype(jnp.bfloat16)
+    )
+    turned[pl.ds(probe_count, 16)] = jnp.ones((16, long), jnp.bfloat16)
+    codes = codes_ref[...].astype(jnp.float32)
+    first_block = (which * half_blocks).astype(jnp.float32)
+    line = lax.broadcasted_iota(jnp.int32, (16, rows), 0).astype(jnp.float32)
+    seen = (line + first_block != codes).astype(jnp.float32)
+    sums = jnp.dot(seen.astype(jnp.bfloat16), probes, preferred_element_type=jnp.float32)
+    counts = jnp.broadcast_to(jnp.sum(seen, 1, keepdims=True), (16, BLOCK_SNPS))
+    out_ref[pl.ds(half + 2 * half_blocks, half_blocks)] = sums[:half_blocks]
+    out_ref[pl.ds(half + 3 * half_blocks, half_blocks)] = counts[:half_blocks]
+    if long > rows:
+        codes = jnp.concatenate([codes, jnp.zeros((1, long - rows), jnp.float32)], 1)
+    code_down[...] = jnp.broadcast_to(codes, (BLOCK_SNPS, long)).T
+
+    for copy in copies_in:
+        copy.wait()
+    for i in range(chunks):
+        kept = []
+        for k in range(2):
+            block = 2 * i + k
+            at = pl.ds(block * BLOCK_SNPS, BLOCK_SNPS)
+            dosage = jnp.where(
+                code_down[pl.ds(0, rows)] != first_block + float(block),
+                held[:, at].astype(jnp.float32),
+                0.0,
+            )
+            out_ref[pl.ds(half + half_blocks + block, 1)] = jnp.sum(
+                dosage * dosage, 0, keepdims=True
+            )
+            kept.append(dosage.astype(jnp.bfloat16))
+        both = padded_rows(jnp.concatenate(kept, 1), long)
+        product = jnp.dot(turned[...], both, preferred_element_type=jnp.float32)
+        for k in range(2):
+            block = 2 * i + k
+            columns = slice(k * BLOCK_SNPS, (k + 1) * BLOCK_SNPS)
+            out_ref[pl.ds(block * BLOCK_SNPS, BLOCK_SNPS)] = product[:probe_count, columns].T
+            out_ref[pl.ds(half + block, 1)] = product[probe_count : probe_count + 1, columns]
+
+
+def moments(which, genotypes, probes, codes, vmem):
+    rows, snps = genotypes.shape
+    half = snps // 2
+    long = -(-rows // PADDED) * PADDED
+    return pl.pallas_call(
+        moments_kernel,
+        in_specs=[
+            pl.BlockSpec(memory_space=pltpu.SMEM),
+            pl.BlockSpec(memory_space=pltpu.HBM),
+            pl.BlockSpec(memory_space=pltpu.VMEM),
+            pl.BlockSpec(memory_space=pltpu.VMEM),
+        ],
+        out_specs=pl.BlockSpec(memory_space=pltpu.VMEM),
+        scratch_shapes=[
+            pltpu.VMEM((rows, half), jnp.bfloat16),
+            pltpu.VMEM((probes.shape[1] + 16, long), jnp.bfloat16),
+            pltpu.VMEM((long, BLOCK_SNPS), jnp.float32),
+            pltpu.SemaphoreType.DMA((PIECES,)),
+        ],
+        out_shape=jax.ShapeDtypeStruct((half + EXTRA, BLOCK_SNPS), jnp.float32),
+        compiler_params=pltpu.CompilerParams(vmem_limit_bytes=vmem * 2**20),
+        cost_estimate=pl.CostEstimate(
+            flops=1_500_000_000, bytes_accessed=3_000_000, transcendentals=0
+        ),
+    )(which.reshape(1), genotypes, probes, codes)
+
+
 def per_device(genotypes, probes, missing_codes):
     rows, snps = genotypes.shape
     probe_count = probes.shape[1]
@@ -145,27 +251,9 @@
     snp_block = jnp.arange(snps) // BLOCK_SNPS
     seen = snp_block[None, :] != missing_codes[:, None]
     observed = seen.astype(jnp.float32)
-    kept = jnp.where(seen, genotypes, jnp.zeros_like(genotypes))
-    dosage = kept.astype(jnp.float32)
-    raw = jnp.einsum("rs,rb->sb", kept, probes, preferred_element_type=jnp.float32)
-    total = jnp.sum(dosage, 0).reshape(blocks, BLOCK_SNPS)
-    square = jnp.sum(dosage * dosage, 0).reshape(blocks, BLOCK_SNPS)
-    by_block = jnp.arange(blocks)[None, :] != missing_codes[:, None]
-    seen_probes = jnp.einsum(
-        "rk,rb->kb", by_block.astype(jnp.bfloat16), probes, preferred_element_type=jnp.float32
-    )
-    count = jnp.broadcast_to(
-        jnp.sum(by_block.astype(jnp.float32), 0)[:, None], (blocks, BLOCK_SNPS)
-    )
-
-    def part(which):
-        def take(a):
-            n = a.shape[0] // 2
-            return lax.dynamic_slice_in_dim(a, which * n, n)
-
-        return jnp.concatenate([take(a) for a in (raw, total, square, seen_probes, count)])
-
-    mine = part(core) + swapped(part(1 - core))
+    codes = missing_codes.reshape(1, rows)
+    sent = moments(1 - core, genotypes, probes, codes, 56)
+    mine = moments(core, genotypes, probes, codes, 32) + swapped(sent)
     mine = summed_everywhere(mine)
     other = swapped(mine)
     first = jnp.where(core == 0, mine, other)
@@ -212,11 +300,11 @@
     inverse = inverse_of_factor(
         1.0 / math.sqrt(snps), gram_of(core, mine), gram_of(1 - core, other)
     )
-    basis = jnp.dot(image.astype(jnp.float32), inverse.T, precision=lax.Precision.HIGHEST)
+    basis = jnp.dot(image.astype(jnp.float32), inverse.T, precision=lax.Precision.HIGH)
     cross = jnp.where(
         core == 0, jnp.concatenate([mine, other]), jnp.concatenate([other, mine])
     )
-    scores = jnp.dot(cross, inverse.T, precision=lax.Precision.HIGHEST)
+    scores = jnp.dot(cross, inverse.T, precision=lax.Precision.HIGH)
     return (
         (basis * math.sqrt(total_rows)).astype(jnp.bfloat16),
         (scores * math.sqrt(snps / total_rows)).astype(jnp.bfloat16),

time: 163 us -> 160 us (0.982)
  Pallas kernels: 6.03 us -> 12.4 us
  other arithmetic: 6.55 us -> 1.8 us
  matrix products: 10.2 us -> 6.94 us
    pallas_call x0 -> x2, Pallas kernels: none -> 6.41 us  [moments(): pl.pallas_call(moments_kernel, in_specs=[pl.BlockSpec(memory_space=pltpu....]
    reduce_sum x6 -> x4, other arithmetic: 5.24 us -> 0.48 us  [the longest x2 0.36 us: summed_everywhere(): shard = jnp.sum(exchanged(blocks_of(array, lax.axis_size(near)), near), 0)]
    dot_general x4 -> x2, matrix products: 5.63 us -> 2.38 us  [the longest x1 1.38 us: per_device(): scores = jnp.dot(cross, inverse.T, precision=lax.Precision.HIGH)]
  transfers between devices with their start and end apart: 4 -> 4, of which waited for: 4 -> 4; matrix products, arithmetic and copies ran while one was open for 0% -> 0% of each run, Pallas kernels for 0% -> 1%
where the time goes in v6:
time: 160 us; the launch traced here: 159 us
  blocking collectives  107 us (67%)
  starting transfers between devices  25.8 us (16%)
  Pallas kernels  12.4 us (8%)
  matrix products  6.94 us (4%)
  waiting for transfers between devices  3.99 us (2%)
  other arithmetic  1.8 us (1%)
    all_to_all x6, blocking collectives, exchanged(): return lax.all_to_all(blocks, axis, 0, 0, tiled=True)  107 us
    ppermute x4, starting transfers between devices, swapped(): return lax.ppermute(array, 'c', SWAP)  25.8 us
    pallas_call x2, Pallas kernels, moments(): pl.pallas_call(moments_kernel, in_specs=[pl.BlockSpec(memory_space=pltpu....  6.41 us
    pallas_call x1, Pallas kernels, inverse_of_factor(): pl.pallas_call(lambda *refs: inverse_kernel(scale, *refs), out_shape=jax....  6.03 us
    ppermute x4, waiting for transfers between devices, swapped(): return lax.ppermute(array, 'c', SWAP)  3.99 us
  transfers between devices with their start and end apart: 4, of which 4 were waited for; matrix products, arithmetic and copies ran while one was open for 0% of the time, Pallas kernels for 1%

profile of v6, /device:TPU:1, one launch (start us, length us, event | category | flops | bytes accessed | tf_op | source)
XLA Modules:
  0.0 159.2 jit_solution(6078902172073766845)
XLA Ops:
  0.6 0.0 copy-start.3
  0.6 0.0 copy-start.2
  0.7 0.0 copy-start
  0.7 4.8 %shard_map.51 = f32[1056,128]{1,0:T(8,128)} custom-call(s32[1]{0:T(128)} %bitcast.2.which_ref, bf16[960,2048]{1,0:T(8,128)(2,1)} %genotypes_ref.3, bf16[960,128]{1,0:T(8,128)(2,1)} %probes_ref.3, s32[1,960]{1,0:T(1,128)} %bitcast.54), custom_call_target="tpu_custom_call" | custom-call | flops 1500000000 | bytes 3000000 | tf_op jit(solution)/shard_map/pallas_call | solution.py:219
  5.5 8.8 %collective-permute-start = (f32[1056,128]{1,0:T(8,128)}, f32[1056,128]{1,0:T(8,128)S(1)}, u32[]{:S(2)}, u32[]{:S(2)}) collective-permute-start(f32[1056,128]{1,0:T(8,128)} %shard_map.51), channel_id=1, source_target_pairs={{0,32},{32,0},{1,33},{33,1},{2,34},{34,2},{3,35},{35,3},{4,36},{36... | collective-permute-start | bytes 1622024 | tf_op jit(solution)/shard_map/ppermute | solution.py:39
  14.3 0.0 copy-done.3
  14.3 0.0 copy-done.2
  14.3 0.0 copy-done
  14.3 1.6 %shard_map.50 = f32[1056,128]{1,0:T(8,128)S(1)} custom-call(s32[1]{0:T(128)} %bitcast.which_ref, bf16[960,2048]{1,0:T(8,128)(2,1)S(1)} %copy-done, bf16[960,128]{1,0:T(8,128)(2,1)S(1)} %copy-done.2, s32[1,960]{1,0:T(1,128)S(1)} %bitcast.55), custom_call_target="tpu_custom_call" | custom-call | flops 1500000000 | bytes 3000000 | tf_op jit(solution)/shard_map/pallas_call | solution.py:219
  15.9 0.1 collective-permute-done
  16.0 0.1 add.35
  16.1 20.9 %all_to_all.30 = f32[32,1,4224]{2,1,0:T(1,128)S(1)} all-to-all(f32[32,1,4224]{2,1,0:T(1,128)S(1)} %bitcast.56), channel_id=1, replica_groups=mesh['z'=8,'c'=2,'y'=8,'x'=4] {'y','x'}, dimensions={0} | all-to-all | bytes 1081344 | tf_op jit(solution)/shard_map/all_to_all | solution.py:17
  37.0 0.3 reduce_sum.36
  37.3 0.1 broadcast_in_dim.8
  37.4 17.9 %all_to_all.31 = f32[8,1,4224]{2,1,0:T(1,128)S(1)} all-to-all(f32[8,1,4224]{2,1,0:T(1,128)S(1)} %broadcast_in_dim.8), channel_id=1, replica_groups=mesh['z'=8,'c'=2,'y'=8,'x'=4] {'z'}, dimensions={0} | all-to-all | bytes 270336 | tf_op jit(solution)/shard_map/all_to_all | solution.py:17
  55.3 0.1 reduce_sum.37
  55.4 0.3 broadcast_in_dim.9
  55.7 18.4 %all_to_all.32 = f32[32,1,4224]{2,1,0:T(1,128)S(1)} all-to-all(f32[32,1,4224]{2,1,0:T(1,128)S(1)} %broadcast_in_dim.9), channel_id=1, replica_groups=mesh['z'=8,'c'=2,'y'=8,'x'=4] {'y','x'}, dimensions={0} | all-to-all | bytes 1081344 | tf_op jit(solution)/shard_map/all_to_all | solution.py:17
  74.1 7.5 %collective-permute-start.1 = (f32[1056,128]{1,0:T(8,128)S(1)}, f32[1056,128]{1,0:T(8,128)S(1)}, u32[]{:S(2)}, u32[]{:S(2)}) collective-permute-start(f32[1056,128]{1,0:T(8,128)S(1)} %bitcast.57), channel_id=1, source_target_pairs={{0,32},{32,0},{1,33},{33,1},{2,34},{34,2},{3,35},{35,3},{4,36},{36... | collective-permute-start | bytes 1622024 | tf_op jit(solution)/shard_map/ppermute | solution.py:39
  81.6 0.0 copy-start.1
  81.6 1.5 collective-permute-done.1
  83.2 0.1 broadcast_select_fusion.1
  83.4 1.1 fusion.5
  84.5 0.0 copy-done.1
  84.5 1.8 %fusion.2 = bf16[960,128]{1,0:T(8,128)(2,1)S(1)} fusion(bf16[2048,128]{1,0:T(8,128)(2,1)S(1)} %fusion.5, bf16[960,2048]{1,0:T(8,128)(2,1)S(1)} %copy-done.1, f32[2048]{0:T(1024)S(1)} %fusion.23, f32[2048]{0:T(1024)S(1)} %fusion.19, s32[2048]{0:T(1024)S(1)} %add_select_fusion, s32[960]{0:T(1024)S(1)} %copy-done.3), kind=kOutput, calls=%fused_computation.6 | convolution fusion | flops 515358720 | bytes 4730624 | tf_op jit(solution)/shard_map/dot_general | solution.py:281
  86.3 1.9 %fusion.16 = f32[2048,128]{1,0:T(8,128)S(1)} fusion(bf16[960,128]{1,0:T(8,128)(2,1)S(1)} %fusion.2, bf16[960,2048]{1,0:T(8,128)(2,1)S(1)} %copy-done.1, f32[2048]{0:T(1024)S(1)} %fusion.23, f32[2048]{0:T(1024)S(1)} %fusion.19, s32[2048]{0:T(1024)S(1)} %add_select_fusion, s32[960]{0:T(1024)S(1)} %copy-done.3), kind=kOutput, calls=%fused_computation.26 | convolution fusion | flops 515112960 | bytes 5254912 | tf_op jit(solution)/shard_map/rs,rb->sb/dot_general | solution.py:283
  88.2 2.3 %collective-permute-start.2 = (f32[1024,128]{1,0:T(8,128)S(1)}, f32[1024,128]{1,0:T(8,128)S(1)}, u32[]{:S(2)}, u32[]{:S(2)}) collective-permute-start(f32[1024,128]{1,0:T(8,128)S(1)} %constant_dynamic-slice_fusion), channel_id=1, source_target_pairs={{0,32},{32,0},{1,33},{33,1},{2,34},{34,2},{3,35},{35,3},{4,36},{36... | collective-permute-start | bytes 1572872 | tf_op jit(solution)/shard_map/ppermute | solution.py:39
  90.5 1.5 collective-permute-done.2
  92.0 0.1 dynamic-slice_add_fusion
  92.1 20.5 %all_to_all.33 = f32[32,32,128]{2,1,0:T(8,128)S(1)} all-to-all(f32[32,32,128]{2,1,0:T(8,128)S(1)} %bitcast.62), channel_id=1, replica_groups=mesh['z'=8,'c'=2,'y'=8,'x'=4] {'y','x'}, dimensions={0} | all-to-all | bytes 1048576 | tf_op jit(solution)/shard_map/all_to_all | solution.py:17
  112.7 10.4 %all_to_all.34 = f32[8,32,128]{2,1,0:T(8,128)S(1)} all-to-all(f32[8,32,128]{2,1,0:T(8,128)S(1)} %broadcast_in_dim.10), channel_id=1, replica_groups=mesh['z'=8,'c'=2,'y'=8,'x'=4] {'z'}, dimensions={0} | all-to-all | bytes 262144 | tf_op jit(solution)/shard_map/all_to_all | solution.py:17
  123.1 0.1 broadcast_in_dim.11
  123.2 18.7 %all_to_all.35 = f32[32,32,128]{2,1,0:T(8,128)S(1)} all-to-all(f32[32,32,128]{2,1,0:T(8,128)S(1)} %broadcast_in_dim.11), channel_id=1, replica_groups=mesh['z'=8,'c'=2,'y'=8,'x'=4] {'y','x'}, dimensions={0} | all-to-all | bytes 1048576 | tf_op jit(solution)/shard_map/all_to_all | solution.py:17
  141.8 7.2 %collective-permute-start.3 = (f32[1024,128]{1,0:T(8,128)S(1)}, f32[1024,128]{1,0:T(8,128)S(1)}, u32[]{:S(2)}, u32[]{:S(2)}) collective-permute-start(f32[1024,128]{1,0:T(8,128)S(1)} %bitcast.59), channel_id=1, source_target_pairs={{0,32},{32,0},{1,33},{33,1},{2,34},{34,2},{3,35},{35,3},{4,36},{36... | collective-permute-start | bytes 1572872 | tf_op jit(solution)/shard_map/ppermute | solution.py:39
  149.0 0.5 fusion.14.refs_0_
  149.5 0.9 collective-permute-done.3
  150.4 0.4 fusion.12.refs_1_
  150.8 6.0 %shard_map.52 = f32[128,128]{1,0:T(8,128)S(1)} custom-call(f32[128,128]{1,0:T(8,128)S(1)} %fusion.14.refs_0_, f32[128,128]{1,0:T(8,128)S(1)} %fusion.12.refs_1_), custom_call_target="tpu_custom_call" | custom-call | flops 6000000000 | bytes 1000000 | tf_op jit(solution)/shard_map/pallas_call | solution.py:127
  156.8 1.0 fusion.1
  157.9 1.4 fusion
  (13 shorter events, 0.2 us)
Async XLA Ops:
  0.6 13.6 %copy-start.3 = (s32[960]{0:T(1024)S(1)}, s32[960]{0:T(1024)}, u32[]{:S(2)}) copy-start(s32[960]{0:T(1024)} %param.5) | copy-start | bytes 11524
  0.6 13.6 %copy-start.2 = (bf16[960,128]{1,0:T(8,128)(2,1)S(1)}, bf16[960,128]{1,0:T(8,128)(2,1)}, u32[]{:S(2)}) copy-start(bf16[960,128]{1,0:T(8,128)(2,1)} %probes_ref.3) | copy-start | bytes 737284
  0.7 13.6 %copy-start = (bf16[960,2048]{1,0:T(8,128)(2,1)S(1)}, bf16[960,2048]{1,0:T(8,128)(2,1)}, u32[]{:S(2)}) copy-start(bf16[960,2048]{1,0:T(8,128)(2,1)} %genotypes_ref.3) | copy-start | bytes 11796484
  5.5 10.5 %collective-permute-start = (f32[1056,128]{1,0:T(8,128)}, f32[1056,128]{1,0:T(8,128)S(1)}, u32[]{:S(2)}, u32[]{:S(2)}) collective-permute-start(f32[1056,128]{1,0:T(8,128)} %shard_map.51), channel_id=1, source_target_pairs={{0,32},{32,0},{1,33},{33,1},{2,34},{34,2},{3,35},{35,3},{4,36},{36... | collective-permute-start | bytes 1622024 | tf_op jit(solution)/shard_map/ppermute | solution.py:39
  74.1 9.1 %collective-permute-start.1 = (f32[1056,128]{1,0:T(8,128)S(1)}, f32[1056,128]{1,0:T(8,128)S(1)}, u32[]{:S(2)}, u32[]{:S(2)}) collective-permute-start(f32[1056,128]{1,0:T(8,128)S(1)} %bitcast.57), channel_id=1, source_target_pairs={{0,32},{32,0},{1,33},{33,1},{2,34},{34,2},{3,35},{35,3},{4,36},{36... | collective-permute-start | bytes 1622024 | tf_op jit(solution)/shard_map/ppermute | solution.py:39
  81.6 2.9 %copy-start.1 = (bf16[960,2048]{1,0:T(8,128)(2,1)S(1)}, bf16[960,2048]{1,0:T(8,128)(2,1)}, u32[]{:S(2)}) copy-start(bf16[960,2048]{1,0:T(8,128)(2,1)} %genotypes_ref.3) | copy-start | bytes 11796484
  88.2 3.8 %collective-permute-start.2 = (f32[1024,128]{1,0:T(8,128)S(1)}, f32[1024,128]{1,0:T(8,128)S(1)}, u32[]{:S(2)}, u32[]{:S(2)}) collective-permute-start(f32[1024,128]{1,0:T(8,128)S(1)} %constant_dynamic-slice_fusion), channel_id=1, source_target_pairs={{0,32},{32,0},{1,33},{33,1},{2,34},{34,2},{3,35},{35,3},{4,36},{36... | collective-permute-start | bytes 1572872 | tf_op jit(solution)/shard_map/ppermute | solution.py:39
  141.8 8.5 %collective-permute-start.3 = (f32[1024,128]{1,0:T(8,128)S(1)}, f32[1024,128]{1,0:T(8,128)S(1)}, u32[]{:S(2)}, u32[]{:S(2)}) collective-permute-start(f32[1024,128]{1,0:T(8,128)S(1)} %bitcast.59), channel_id=1, source_target_pairs={{0,32},{32,0},{1,33},{33,1},{2,34},{34,2},{3,35},{35,3},{4,36},{36... | collective-permute-start | bytes 1572872 | tf_op jit(solution)/shard_map/ppermute | solution.py:39
